TPU v7x, 256 devices: a whole 4x4x8 slice. The times are simulated.
256 devices in a mesh: row: 8 (over z_lo, core), col: 32 (over y, z_hi, x).
Axes of the slice: x: 4, y: 4, z: 8 (z_hi: 2, z_lo: 4; z = z_hi * 4 + z_lo), core: 2. Of those that a mesh axis runs over, the one named last changes fastest.
Arguments:
- amplitudes: bfloat16 [8, 512, 4096], P(None, 'col', 'row'), may hold values from -6 to 6
- integrals: bfloat16 [8, 4096, 32768], P('row', None, 'col'), may hold values from -0.125 to 0.125
- bare: bfloat16 [8, 512, 32768], P('row', None, 'col'), may hold values from -6 to 6
- cd_count: int32 [8], replicated, may hold values from 1 to 4096, 20480 in all
- ij_orbitals: int32 [8, 2, 512], P('row'), may hold values from 0 to 199
- ab_orbitals: int32 [8, 2, 32768], P('row', None, 'col'), may hold values from 0 to 1799
- occ_energy: float32 [200], replicated, may hold values from -2 to -0.5
- vir_energy: float32 [1800], replicated, may hold values from 0.5 to 3
Outputs:
- updated: float32 [8, 512, 32768], P('row', None, 'col')
Inputs may be any that keep to these rules, and one draw needn't show every extreme that they name: Each irrep's live pairs cd are the first cd_count of its 4096 slots; some irrep has all 4096, and the counts sum to 20480.
All inputs are finite; a program needn't handle non-finite values.
Results may differ from a plain program's by a relative error of at most 0.0003.
Values may be sent and summed in bfloat16 or wider, within the bound.
No kernel may reach another device: no remote copies, remote signals or barrier semaphores. Data moves between devices by JAX's collectives and lax.ppermute only.
A program may use at most 64 MiB of HBM per device.

v0:
```python
import jax
import jax.numpy as jnp
from jax import lax
from jax.sharding import PartitionSpec as P


def on_device(
    amplitudes, integrals, bare, cd_count, ij_orbitals, ab_orbitals, occ_energy, vir_energy
):
    held_irreps = integrals.shape[0]
    slots = integrals.shape[1]
    first_irrep = lax.axis_index("row") * held_irreps
    counts = lax.dynamic_slice_in_dim(cd_count, first_irrep, held_irreps, 0)
    positions = jnp.arange(slots, dtype=jnp.int32)
    gathered = lax.all_gather(amplitudes, "col", axis=1, tiled=True)
    owned = lax.all_to_all(gathered, "row", split_axis=0, concat_axis=2, tiled=True)
    ladder = jnp.einsum(
        "hic,hca->hia",
        jnp.where(positions[None, None, :] < counts[:, None, None], owned, jnp.zeros_like(owned)),
        integrals,
        preferred_element_type=jnp.float32,
    )
    residual = bare.astype(jnp.float32) + 0.5 * ladder
    occ_sum = jnp.take(occ_energy, ij_orbitals[:, 0, :]) + jnp.take(
        occ_energy, ij_orbitals[:, 1, :]
    )
    vir_sum = jnp.take(vir_energy, ab_orbitals[:, 0, :]) + jnp.take(
        vir_energy, ab_orbitals[:, 1, :]
    )
    return residual / (vir_sum[:, None, :] - occ_sum[:, :, None])


def solution(mesh):
    return jax.shard_map(
        on_device,
        mesh=mesh,
        in_specs=(
            P(None, "col", "row"),
            P("row", None, "col"),
            P("row", None, "col"),
            P(),
            P("row", None, None),
            P("row", None, "col"),
            P(),
            P(),
        ),
        out_specs=P("row", None, "col"),
        check_vma=False,
    )
```

profile of v0, /device:TPU:8, one launch (start us, length us, event | category | flops | bytes accessed | tf_op | source)
XLA Modules:
  0.0 249.4 jit_solution(11903524399670531882)
XLA Ops:
  6.5 0.0 copy-start
  6.5 0.0 all-gather.2.cloned.1.call-start
  6.5 1.6 copy.10
  8.2 0.0 all-gather.2.cloned.1.call-update
  8.2 116.0 %all-gather.2.cloned.1.call-done = bf16[8,512,512]{2,0,1:T(8,128)(2,1)} async-done(((bf16[8,16,512]{2,0,1:T(8,128)(2,1)}), bf16[8,512,512]{2,0,1:T(8,128)(2,1)}) %all-gather.2.cloned.1.call-update) | async-done | bytes 4194320 | tf_op jit(solution)/shard_map/all_gather | solution.py:15
  124.2 7.5 %copy.11 = bf16[8,512,512]{1,2,0:T(8,128)(2,1)} copy(bf16[8,512,512]{2,0,1:T(8,128)(2,1)} %all-gather.2.cloned.1.call-done) | data formatting | bytes 8388608 | tf_op jit(solution)/shard_map/all_gather | solution.py:15
  131.8 0.0 copy-start.3
  131.8 0.0 copy-start.1
  131.8 4.7 %all-to-all-start = ((bf16[8,512,512]{1,2,0:T(8,128)(2,1)}), bf16[8,512,512]{1,2,0:T(8,128)(2,1)}, u32[]{:S(2)}, u32[]{:S(2)}) async-start(bf16[8,512,512]{1,2,0:T(8,128)(2,1)} %copy.11), calls=%async_computation | async-start | bytes 8388608 | tf_op jit(solution)/shard_map/all_to_all | solution.py:16
  136.5 0.0 copy-start.2
  136.5 0.0 copy-done.3
  136.5 0.0 copy-done.1
  136.6 3.5 %gather_fusion.2 = f32[512]{0:T(512)S(1)} fusion(f32[200]{0:T(256)S(1)} %copy-done.1, s32[1024]{0:T(1024)S(1)} %pad_clamp_fusion.1), kind=kCustom, calls=%fused_computation.1.clone | custom fusion | bytes 6144 | tf_op jit(solution)/shard_map/jit(_take)/gather | solution.py:24
  140.1 3.5 %gather_fusion.3 = f32[512]{0:T(512)S(1)} fusion(f32[200]{0:T(256)S(1)} %copy-done.1, s32[1024]{0:T(1024)S(1)} %pad_clamp_fusion), kind=kCustom, calls=%fused_computation.3.clone | custom fusion | bytes 6144 | tf_op jit(solution)/shard_map/jit(_take)/gather | solution.py:24
  143.6 0.0 copy-done.2
  143.6 0.0 copy-done
  143.6 0.0 copy-start.5
  143.6 6.2 %gather_fusion = f32[1024]{0:T(1024)S(1)} fusion(f32[1800]{0:T(1024)S(1)} %copy-done, s32[1024]{0:T(1024)S(1)} %broadcast_clamp_fusion.1), kind=kCustom, calls=%fused_computation.clone | custom fusion | bytes 12288 | tf_op jit(solution)/shard_map/jit(_take)/gather | solution.py:27
  149.8 6.2 %gather_fusion.1 = f32[1024]{0:T(1024)S(1)} fusion(f32[1800]{0:T(1024)S(1)} %copy-done, s32[1024]{0:T(1024)S(1)} %broadcast_clamp_fusion), kind=kCustom, calls=%fused_computation.2.clone | custom fusion | bytes 12288 | tf_op jit(solution)/shard_map/jit(_take)/gather | solution.py:27
  156.0 0.0 copy-done.5
  156.0 0.6 dynamic_slice.3
  156.6 0.7 add_compare_fusion
  157.3 0.0 copy-start.4
  157.3 73.2 %all-to-all-done = bf16[8,512,512]{1,2,0:T(8,128)(2,1)} async-done(((bf16[8,512,512]{1,2,0:T(8,128)(2,1)}), bf16[8,512,512]{1,2,0:T(8,128)(2,1)}, u32[]{:S(2)}, u32[]{:S(2)}) %all-to-all-start) | async-done | bytes 4194336 | tf_op jit(solution)/shard_map/all_to_all | solution.py:16
  230.5 2.6 %bitcast_select_fusion = bf16[8,1,512,512]{2,3,0,1:T(8,128)(2,1)S(1)} fusion(bf16[8,512,512]{1,2,0:T(8,128)(2,1)} %all-to-all-done, pred[8,512]{1,0:T(8,128)(4,1)S(1)} %add_compare_fusion), kind=kLoop, calls=%fused_computation.6 | loop fusion | flops 2097152 | bytes 8392704 | tf_op jit(solution)/shard_map/jit(_where)/select_n | solution.py:19
  233.1 0.0 copy-done.4
  233.1 9.4 %fusion.2 = f32[1,512,1024]{2,1,0:T(8,128)} fusion(bf16[1,512,1024]{2,1,0:T(8,128)(2,1)S(1)} %copy-done.4, bf16[512,4096]{0,1:T(8,128)(2,1)S(1)} %bitcast.42, bf16[1,4096,1024]{2,1,0:T(8,128)(2,1)} %param.13, f32[512]{0:T(512)S(1)} %bitcast.52, f32[1024]{0:T(1024)S(1)} %bitcast.51), kind=kOutput, calls=%fused_computation.8 | convolution fusion | flops 4297588736 | bytes 15734784 | tf_op jit(solution)/shard_map/hic,hca->hia/dot_general | solution.py:17
  (8 shorter events, 0.1 us)
Async XLA Ops:
  6.5 137.1 %copy-start = (f32[1800]{0:T(1024)S(1)}, f32[1800]{0:T(1024)}, u32[]{:S(2)}) copy-start(f32[1800]{0:T(1024)} %param.19) | copy-start | bytes 21604
  6.5 117.7 %all-gather.2.cloned.1.call-start = ((), (), s32[]{:S(2)}) async-start(), calls=%async_computation.1 | async-start | bytes 4325376 | tf_op jit(solution)/shard_map/all_gather | solution.py:15
  131.8 4.7 %copy-start.3 = (s32[1,2,512]{2,1,0:T(2,128)S(1)}, s32[1,2,512]{2,1,0:T(2,128)}, u32[]{:S(2)}) copy-start(s32[1,2,512]{2,1,0:T(2,128)} %param.16) | copy-start | bytes 12292
  131.8 4.8 %copy-start.1 = (f32[200]{0:T(256)S(1)}, f32[200]{0:T(256)}, u32[]{:S(2)}) copy-start(f32[200]{0:T(256)} %param.18) | copy-start | bytes 2404
  131.8 98.7 %all-to-all-start = ((bf16[8,512,512]{1,2,0:T(8,128)(2,1)}), bf16[8,512,512]{1,2,0:T(8,128)(2,1)}, u32[]{:S(2)}, u32[]{:S(2)}) async-start(bf16[8,512,512]{1,2,0:T(8,128)(2,1)} %copy.11), calls=%async_computation | async-start | bytes 8388608 | tf_op jit(solution)/shard_map/all_to_all | solution.py:16
  136.5 7.1 %copy-start.2 = (s32[1,2,1024]{2,1,0:T(2,128)S(1)}, s32[1,2,1024]{2,1,0:T(2,128)}, u32[]{:S(2)}) copy-start(s32[1,2,1024]{2,1,0:T(2,128)} %param.17) | copy-start | bytes 24580
  143.6 12.3 %copy-start.5 = (s32[8]{0:T(128)S(1)}, s32[8]{0:T(128)}, u32[]{:S(2)}) copy-start(s32[8]{0:T(128)} %param.15) | copy-start | bytes 100
  157.3 75.8 %copy-start.4 = (bf16[1,512,1024]{2,1,0:T(8,128)(2,1)S(1)}, bf16[1,512,1024]{2,1,0:T(8,128)(2,1)}, u32[]{:S(2)}) copy-start(bf16[1,512,1024]{2,1,0:T(8,128)(2,1)} %param.14) | copy-start | bytes 3145732
Sparse Core Ops, SparseCore 0:
  10.8 113.4 all-gather.1
where the time goes:
time: 252 us; the launch traced here: 249 us
  waiting for transfers between devices  189 us (75%)
  local copies, waits for them, and re-layouts  29.1 us (12%)
  between operations  13.6 us (5%)
  matrix products  9.43 us (4%)
  starting transfers between devices  4.69 us (2%)
  other arithmetic  3.32 us (1%)
    all_gather x1, waiting for transfers between devices, on_device(): gathered = lax.all_gather(amplitudes, 'col', axis=1, tiled=True)  116 us
    all_to_all x1, waiting for transfers between devices, on_device(): lax.all_to_all(gathered, 'row', split_axis=0, concat_axis=2, tiled=True)  73.2 us
    dot_general x1, matrix products, on_device(): jnp.einsum('hic,hca->hia', jnp.where(positions[None, None, :] < counts[:,...  9.43 us
    all_gather x1, local copies, waits for them, and re-layouts, on_device(): gathered = lax.all_gather(amplitudes, 'col', axis=1, tiled=True)  7.55 us
    gather x1, local copies, waits for them, and re-layouts, on_device(): jnp.take(vir_energy, ab_orbitals[:, 0, :])  6.15 us
    gather x1, local copies, waits for them, and re-layouts, on_device(): jnp.take(vir_energy, ab_orbitals[:, 1, :])  6.15 us
  transfers between devices with their start and end apart: 2, of which 2 were waited for; matrix products, arithmetic and copies ran while one was open for 8% of the time, Pallas kernels for 0%

commit v1 on v0

v1 whole, which is shorter than its diff:
```python
import functools

import jax
import jax.numpy as jnp
from jax import lax
from jax.experimental import pallas as pl
from jax.experimental.pallas import tpu as pltpu
from jax.sharding import PartitionSpec as P

NY, NZ, NX = 4, 2, 4
TILE = 256


def moves(axis, shift):
    pairs = []
    for y in range(NY):
        for z in range(NZ):
            for x in range(NX):
                ty, tz, tx = y, z, x
                if axis == "y":
                    ty = (y + shift) % NY
                elif axis == "x":
                    tx = (x + shift) % NX
                else:
                    tz = (z + shift) % NZ
                pairs.append(((y * NZ + z) * NX + x, (ty * NZ + tz) * NX + tx))
    return pairs


def send(block, axis, shift):
    return lax.ppermute(block, "col", moves(axis, shift))


def near(block, axis):
    back = send(block, axis, 1)
    ahead = send(block, axis, -1)
    far = send(block, axis, 2)
    return jnp.stack([block, back, ahead, far])


def wide(blocks, axis):
    back = send(blocks, axis, 1)
    ahead = send(blocks, axis, -1)
    far_low = send(back[:2], axis, 1)
    far_high = send(ahead[2:], axis, -1)
    return [(blocks, 0, 0), (back, 3, 0), (ahead, 1, 0), (far_low, 2, 0), (far_high, 2, 2)]


NEAR = (0, 3, 1, 2)


def ladder_kernel(layout, place_ref, *refs):
    count = len(layout)
    pieces = refs[:count]
    integrals_ref, bare_ref, ij_ref, ab_ref, occ_ref, vir_ref, out_ref, live_ref, occ_col_ref = refs[count:]

    @pl.when(pl.program_id(0) == 0)
    def _():
        y, z, x = place_ref[0], place_ref[1], place_ref[2]
        for ref, (zs, dy0, dx0, panel, kind) in zip(pieces, layout):
            for k in range(ref.shape[0]):
                if kind == "xy":
                    dy, dx = dy0, NEAR[dx0 + k]
                else:
                    dy, dx = NEAR[dy0 + k], dx0
                row = (((y + dy) % NY) * NZ + (z + zs) % NZ) * NX + (x + dx) % NX
                row = pl.multiple_of(row * 16, 16)
                for p in range(ref.shape[1]):
                    live_ref[pl.ds(row, 16), (panel + p) * 512 : (panel + p + 1) * 512] = ref[k, p]
        for s in range(4):
            occ = jnp.zeros((8, 128), jnp.float32)
            for side in range(2):
                index = jnp.broadcast_to(ij_ref[0, side : side + 1, s * 128 : (s + 1) * 128], (8, 128))
                occ = occ + pick(occ_ref, index)
            occ_col_ref[s * 128 : (s + 1) * 128, :] = jnp.broadcast_to(occ[:1], (128, 128)).T

    ladder = jnp.dot(live_ref[...], integrals_ref[0], preferred_element_type=jnp.float32)
    for s in range(TILE // 128):
        cols = slice(s * 128, (s + 1) * 128)
        vir = jnp.zeros((8, 128), jnp.float32)
        for side in range(2):
            vir = vir + pick(vir_ref, jnp.broadcast_to(ab_ref[0, side : side + 1, cols], (8, 128)))
        residual = bare_ref[0, :, cols].astype(jnp.float32) + 0.5 * ladder[:, cols]
        out_ref[0, :, cols] = residual / (vir[:1] - occ_col_ref[...])


def pick(table_ref, index):
    rows = table_ref.shape[0]
    high, low = index >> 7, index & 127
    got = jnp.zeros((8, 128), jnp.float32)
    for r in range(rows):
        row = jnp.broadcast_to(table_ref[r : r + 1, :], (8, 128))
        got = jnp.where(high == r, jnp.take_along_axis(row, low, axis=1), got)
    return got


def on_device(
    amplitudes, integrals, bare, cd_count, ij_orbitals, ab_orbitals, occ_energy, vir_energy
):
    width = amplitudes.shape[2]
    positions = lax.axis_index("row") * width + jnp.arange(width, dtype=jnp.int32)
    live = jnp.where(
        positions[None, None, :] < cd_count[:, None, None], amplitudes, jnp.zeros_like(amplitudes)
    )
    own = lax.all_to_all(live, "row", split_axis=0, concat_axis=0, tiled=True)
    other = send(own, "z", 1)
    pieces, layout = [], []
    for zs, block in ((0, own), (1, other)):
        for part, dy_first in ((0, False), (1, True)):
            half = block[part * 4 : part * 4 + 4]
            first, second = ("y", "x") if dy_first else ("x", "y")
            for array, shift, begin in wide(near(half, first), second):
                pieces.append(array)
                if dy_first:
                    layout.append((zs, begin, shift, part * 4, "yx"))
                else:
                    layout.append((zs, shift, begin, part * 4, "xy"))
    occ_table = jnp.pad(occ_energy, (0, 56)).reshape(2, 128)
    vir_table = jnp.pad(vir_energy, (0, 120)).reshape(15, 128)
    col = lax.axis_index("col")
    place = jnp.stack([col // (NZ * NX), (col // NX) % NZ, col % NX]).astype(jnp.int32)

    def whole(array):
        return pl.BlockSpec(array.shape, lambda n, place, r=array.ndim: (0,) * r)

    return pl.pallas_call(
        functools.partial(ladder_kernel, tuple(layout)),
        grid_spec=pltpu.PrefetchScalarGridSpec(
            num_scalar_prefetch=1,
            grid=(1024 // TILE,),
            in_specs=[whole(p) for p in pieces]
            + [
                pl.BlockSpec((1, 4096, TILE), lambda n, place: (0, 0, n)),
                pl.BlockSpec((1, 512, TILE), lambda n, place: (0, 0, n)),
                whole(ij_orbitals),
                pl.BlockSpec((1, 2, TILE), lambda n, place: (0, 0, n)),
                whole(occ_table),
                whole(vir_table),
            ],
            out_specs=pl.BlockSpec((1, 512, TILE), lambda n, place: (0, 0, n)),
            scratch_shapes=[pltpu.VMEM((512, 4096), jnp.bfloat16), pltpu.VMEM((512, 128), jnp.float32)],
        ),
        out_shape=jax.ShapeDtypeStruct((1, 512, 1024), jnp.float32),
        compiler_params=pltpu.CompilerParams(vmem_limit_bytes=48 * 1024 * 1024),
    )(place, *pieces, integrals, bare, ij_orbitals, ab_orbitals, occ_table, vir_table)


def solution(mesh):
    return jax.shard_map(
        on_device,
        mesh=mesh,
        in_specs=(
            P(None, "col", "row"),
            P("row", None, "col"),
            P("row", None, "col"),
            P(),
            P("row", None, None),
            P("row", None, "col"),
            P(),
            P(),
        ),
        out_specs=P("row", None, "col"),
        check_vma=False,
    )
```

time: 252 us -> 90.2 us (0.36)
  the two profiles are of different devices: /device:TPU:8 before, /device:TPU:24 now
where the time goes in v1:
time: 90.2 us; the launch traced here: 89.8 us
  starting transfers between devices  46.9 us (52%)
  waiting for transfers between devices  13.3 us (15%)
  blocking collectives  12.5 us (14%)
  Pallas kernels  9.1 us (10%)
  local copies, waits for them, and re-layouts  6.06 us (7%)
  other arithmetic  1.87 us (2%)
    ppermute x29, starting transfers between devices, send(): return lax.ppermute(block, 'col', moves(axis, shift))  46.9 us
    ppermute x29, waiting for transfers between devices, send(): return lax.ppermute(block, 'col', moves(axis, shift))  13.3 us
    all_to_all x1, blocking collectives, on_device(): own = lax.all_to_all(live, 'row', split_axis=0, concat_axis=0, tiled=True)  12.5 us
    pallas_call x1, Pallas kernels, on_device(): pl.pallas_call(functools.partial(ladder_kernel, tuple(layout)), grid_spec...  9.1 us
    unnamed x6, local copies, waits for them, and re-layouts  2.61 us
  transfers between devices with their start and end apart: 29, of which 9 were waited for; matrix products, arithmetic and copies ran while one was open for 4% of the time, Pallas kernels for 0%

profile of v1, /device:TPU:24, one launch (start us, length us, event | category | flops | bytes accessed | tf_op | source)
XLA Modules:
  0.0 89.8 jit_solution(4657769066003976836)
XLA Ops:
  0.0 0.7 broadcast_compare_fusion
  0.7 0.9 %broadcast_select_fusion = bf16[8,16,512]{2,1,0:T(8,128)(2,1)S(1)} fusion(bf16[8,16,512]{2,1,0:T(8,128)(2,1)} %param.8, pred[8,512]{1,0:T(8,128)(4,1)S(1)} %broadcast_compare_fusion), kind=kLoop, calls=%fused_computation.4 | loop fusion | flops 65536 | bytes 266240 | tf_op jit(solution)/shard_map/jit(_where)/select_n | solution.py:102
  1.7 12.5 %all_to_all.5 = bf16[8,16,512]{2,1,0:T(8,128)(2,1)S(1)} all-to-all(bf16[8,16,512]{2,1,0:T(8,128)(2,1)S(1)} %broadcast_select_fusion), channel_id=1, replica_groups=mesh['row'=8,'col'=32] {'row'}, dimensions={0} | all-to-all | bytes 262144 | tf_op jit(solution)/shard_map/all_to_all | solution.py:105
  14.1 4.5 %collective-permute-start.14 = (bf16[8,16,512]{2,1,0:T(8,128)(2,1)S(1)}, bf16[8,16,512]{2,1,0:T(8,128)(2,1)S(1)}, u32[]{:S(2)}, u32[]{:S(2)}) collective-permute-start(bf16[8,16,512]{2,1,0:T(8,128)(2,1)S(1)} %all_to_all.5), channel_id=1, source_target_pairs={{0,4},{1,5},{2,6},{3,7},{4,0},{5,1},{6,2},{7,3},{8,12},{9,13},{10,... | collective-permute-start | bytes 393224 | tf_op jit(solution)/shard_map/ppermute | solution.py:31
  18.7 0.8 collective-permute-start.8
  19.5 2.5 %collective-permute-start.7 = (bf16[4,16,512]{2,1,0:T(8,128)(2,1)S(1)}, bf16[4,16,512]{2,1,0:T(8,128)(2,1)S(1)}, u32[]{:S(2)}, u32[]{:S(2)}) collective-permute-start(bf16[4,16,512]{2,1,0:T(8,128)(2,1)S(1)} %get-tuple-element.11), channel_id=1, source_target_pairs={{0,8},{1,9},{2,10},{3,11},{4,12},{5,13},{6,14},{7,15},{8,16},{9,17... | collective-permute-start | bytes 196616 | tf_op jit(solution)/shard_map/ppermute | solution.py:31
  22.0 2.8 %collective-permute-start.1 = (bf16[4,16,512]{2,1,0:T(8,128)(2,1)S(1)}, bf16[4,16,512]{2,1,0:T(8,128)(2,1)S(1)}, u32[]{:S(2)}, u32[]{:S(2)}) collective-permute-start(bf16[4,16,512]{2,1,0:T(8,128)(2,1)S(1)} %get-tuple-element.12), channel_id=1, source_target_pairs={{0,3},{1,0},{2,1},{3,2},{4,7},{5,4},{6,5},{7,6},{8,11},{9,8},{10,9... | collective-permute-start | bytes 196616 | tf_op jit(solution)/shard_map/ppermute | solution.py:31
  24.7 1.1 %collective-permute-done.14 = bf16[8,16,512]{2,1,0:T(8,128)(2,1)S(1)} collective-permute-done((bf16[8,16,512]{2,1,0:T(8,128)(2,1)S(1)}, bf16[8,16,512]{2,1,0:T(8,128)(2,1)S(1)}, u32[]{:S(2)}, u32[]{:S(2)}) %collective-permute-start.14) | collective-permute-done | bytes 131104 | tf_op jit(solution)/shard_map/ppermute | solution.py:31
  25.8 3.0 %collective-permute-start.2 = (bf16[4,16,512]{2,1,0:T(8,128)(2,1)S(1)}, bf16[4,16,512]{2,1,0:T(8,128)(2,1)S(1)}, u32[]{:S(2)}, u32[]{:S(2)}) collective-permute-start(bf16[4,16,512]{2,1,0:T(8,128)(2,1)S(1)} %get-tuple-element.12), channel_id=1, source_target_pairs={{0,2},{1,3},{2,0},{3,1},{4,6},{5,7},{6,4},{7,5},{8,10},{9,11},{10,... | collective-permute-start | bytes 196616 | tf_op jit(solution)/shard_map/ppermute | solution.py:31
  28.9 1.3 %collective-permute-start.9 = (bf16[4,16,512]{2,1,0:T(8,128)(2,1)S(1)}, bf16[4,16,512]{2,1,0:T(8,128)(2,1)S(1)}, u32[]{:S(2)}, u32[]{:S(2)}) collective-permute-start(bf16[4,16,512]{2,1,0:T(8,128)(2,1)S(1)} %get-tuple-element.11), channel_id=1, source_target_pairs={{0,16},{1,17},{2,18},{3,19},{4,20},{5,21},{6,22},{7,23},{8,24},{9,... | collective-permute-start | bytes 196616 | tf_op jit(solution)/shard_map/ppermute | solution.py:31
  30.2 1.4 %collective-permute-done.2 = bf16[4,16,512]{2,1,0:T(8,128)(2,1)S(1)} collective-permute-done((bf16[4,16,512]{2,1,0:T(8,128)(2,1)S(1)}, bf16[4,16,512]{2,1,0:T(8,128)(2,1)S(1)}, u32[]{:S(2)}, u32[]{:S(2)}) %collective-permute-start.2) | collective-permute-done | bytes 65568 | tf_op jit(solution)/shard_map/ppermute | solution.py:31
  31.6 0.9 %collective-permute-start.4 = (bf16[4,4,16,512]{3,2,1,0:T(8,128)(2,1)S(1)}, bf16[4,4,16,512]{3,2,1,0:T(8,128)(2,1)S(1)}, u32[]{:S(2)}, u32[]{:S(2)}) collective-permute-start(bf16[4,4,16,512]{3,2,1,0:T(8,128)(2,1)S(1)} %pad_maximum_fusion.refs_0_), channel_id=1, source_target_pairs={{0,24},{1,25},{2,26},{3,27},{4,28},{5,29},{6,30},{7,31},{8,0},{9,1... | collective-permute-start | bytes 786440 | tf_op jit(solution)/shard_map/ppermute | solution.py:31
  32.6 2.4 %collective-permute-start.3 = (bf16[4,4,16,512]{3,2,1,0:T(8,128)(2,1)S(1)}, bf16[4,4,16,512]{3,2,1,0:T(8,128)(2,1)S(1)}, u32[]{:S(2)}, u32[]{:S(2)}) collective-permute-start(bf16[4,4,16,512]{3,2,1,0:T(8,128)(2,1)S(1)} %pad_maximum_fusion.refs_0_), channel_id=1, source_target_pairs={{0,8},{1,9},{2,10},{3,11},{4,12},{5,13},{6,14},{7,15},{8,16},{9,17... | collective-permute-start | bytes 786440 | tf_op jit(solution)/shard_map/ppermute | solution.py:31
  35.0 2.8 %collective-permute-start.16 = (bf16[4,16,512]{2,1,0:T(8,128)(2,1)S(1)}, bf16[4,16,512]{2,1,0:T(8,128)(2,1)S(1)}, u32[]{:S(2)}, u32[]{:S(2)}) collective-permute-start(bf16[4,16,512]{2,1,0:T(8,128)(2,1)S(1)} %get-tuple-element.8), channel_id=1, source_target_pairs={{0,3},{1,0},{2,1},{3,2},{4,7},{5,4},{6,5},{7,6},{8,11},{9,8},{10,9... | collective-permute-start | bytes 196616 | tf_op jit(solution)/shard_map/ppermute | solution.py:31
  37.7 2.3 %collective-permute-start.17 = (bf16[4,16,512]{2,1,0:T(8,128)(2,1)S(1)}, bf16[4,16,512]{2,1,0:T(8,128)(2,1)S(1)}, u32[]{:S(2)}, u32[]{:S(2)}) collective-permute-start(bf16[4,16,512]{2,1,0:T(8,128)(2,1)S(1)} %get-tuple-element.8), channel_id=1, source_target_pairs={{0,2},{1,3},{2,0},{3,1},{4,6},{5,7},{6,4},{7,5},{8,10},{9,11},{10,... | collective-permute-start | bytes 196616 | tf_op jit(solution)/shard_map/ppermute | solution.py:31
  40.2 3.7 %collective-permute-start.11 = (bf16[4,4,16,512]{3,2,1,0:T(8,128)(2,1)S(1)}, bf16[4,4,16,512]{3,2,1,0:T(8,128)(2,1)S(1)}, u32[]{:S(2)}, u32[]{:S(2)}) collective-permute-start(bf16[4,4,16,512]{3,2,1,0:T(8,128)(2,1)S(1)} %pad_maximum_fusion.1.refs_5_), channel_id=1, source_target_pairs={{0,3},{1,0},{2,1},{3,2},{4,7},{5,4},{6,5},{7,6},{8,11},{9,8},{10,9... | collective-permute-start | bytes 786440 | tf_op jit(solution)/shard_map/ppermute | solution.py:31
  44.0 1.5 %collective-permute-start.24 = (bf16[4,16,512]{2,1,0:T(8,128)(2,1)S(1)}, bf16[4,16,512]{2,1,0:T(8,128)(2,1)S(1)}, u32[]{:S(2)}, u32[]{:S(2)}) collective-permute-start(bf16[4,16,512]{2,1,0:T(8,128)(2,1)S(1)} %get-tuple-element.7), channel_id=1, source_target_pairs={{0,16},{1,17},{2,18},{3,19},{4,20},{5,21},{6,22},{7,23},{8,24},{9,... | collective-permute-start | bytes 196616 | tf_op jit(solution)/shard_map/ppermute | solution.py:31
  45.6 3.3 %collective-permute-done.22 = bf16[4,16,512]{2,1,0:T(8,128)(2,1)S(1)} collective-permute-done((bf16[4,16,512]{2,1,0:T(8,128)(2,1)S(1)}, bf16[4,16,512]{2,1,0:T(8,128)(2,1)S(1)}, u32[]{:S(2)}, u32[]{:S(2)}) %collective-permute-start.22) | collective-permute-done | bytes 65568 | tf_op jit(solution)/shard_map/ppermute | solution.py:31
  48.9 1.7 %collective-permute-done.24 = bf16[4,16,512]{2,1,0:T(8,128)(2,1)S(1)} collective-permute-done((bf16[4,16,512]{2,1,0:T(8,128)(2,1)S(1)}, bf16[4,16,512]{2,1,0:T(8,128)(2,1)S(1)}, u32[]{:S(2)}, u32[]{:S(2)}) %collective-permute-start.24) | collective-permute-done | bytes 65568 | tf_op jit(solution)/shard_map/ppermute | solution.py:31
  50.5 1.2 %collective-permute-start.19 = (bf16[4,4,16,512]{3,2,1,0:T(8,128)(2,1)S(1)}, bf16[4,4,16,512]{3,2,1,0:T(8,128)(2,1)S(1)}, u32[]{:S(2)}, u32[]{:S(2)}) collective-permute-start(bf16[4,4,16,512]{3,2,1,0:T(8,128)(2,1)S(1)} %pad_maximum_fusion.2.refs_10_), channel_id=1, source_target_pairs={{0,24},{1,25},{2,26},{3,27},{4,28},{5,29},{6,30},{7,31},{8,0},{9,1... | collective-permute-start | bytes 786440 | tf_op jit(solution)/shard_map/ppermute | solution.py:31
  51.8 2.0 %collective-permute-start.18 = (bf16[4,4,16,512]{3,2,1,0:T(8,128)(2,1)S(1)}, bf16[4,4,16,512]{3,2,1,0:T(8,128)(2,1)S(1)}, u32[]{:S(2)}, u32[]{:S(2)}) collective-permute-start(bf16[4,4,16,512]{3,2,1,0:T(8,128)(2,1)S(1)} %pad_maximum_fusion.2.refs_10_), channel_id=1, source_target_pairs={{0,8},{1,9},{2,10},{3,11},{4,12},{5,13},{6,14},{7,15},{8,16},{9,17... | collective-permute-start | bytes 786440 | tf_op jit(solution)/shard_map/ppermute | solution.py:31
  53.8 2.2 %collective-permute-start.26 = (bf16[4,4,16,512]{3,2,1,0:T(8,128)(2,1)S(1)}, bf16[4,4,16,512]{3,2,1,0:T(8,128)(2,1)S(1)}, u32[]{:S(2)}, u32[]{:S(2)}) collective-permute-start(bf16[4,4,16,512]{3,2,1,0:T(8,128)(2,1)S(1)} %pad_maximum_fusion.3.refs_15_), channel_id=1, source_target_pairs={{0,3},{1,0},{2,1},{3,2},{4,7},{5,4},{6,5},{7,6},{8,11},{9,8},{10,9... | collective-permute-start | bytes 786440 | tf_op jit(solution)/shard_map/ppermute | solution.py:31
  58.2 3.0 %collective-permute-start.5 = (bf16[2,4,16,512]{3,2,1,0:T(8,128)(2,1)}, bf16[2,4,16,512]{3,2,1,0:T(8,128)(2,1)S(1)}, u32[]{:S(2)}, u32[]{:S(2)}) collective-permute-start(bf16[2,4,16,512]{3,2,1,0:T(8,128)(2,1)} %slice.49), channel_id=1, source_target_pairs={{0,8},{1,9},{2,10},{3,11},{4,12},{5,13},{6,14},{7,15},{8,16},{9,17... | collective-permute-start | bytes 393224 | tf_op jit(solution)/shard_map/ppermute | solution.py:31
  61.2 3.2 %collective-permute-start.13 = (bf16[2,4,16,512]{3,2,1,0:T(8,128)(2,1)}, bf16[2,4,16,512]{3,2,1,0:T(8,128)(2,1)S(1)}, u32[]{:S(2)}, u32[]{:S(2)}) collective-permute-start(bf16[2,4,16,512]{3,2,1,0:T(8,128)(2,1)} %slice.53), channel_id=1, source_target_pairs={{0,3},{1,0},{2,1},{3,2},{4,7},{5,4},{6,5},{7,6},{8,11},{9,8},{10,9... | collective-permute-start | bytes 393224 | tf_op jit(solution)/shard_map/ppermute | solution.py:31
  65.4 3.3 %collective-permute-start.20 = (bf16[2,4,16,512]{3,2,1,0:T(8,128)(2,1)S(1)}, bf16[2,4,16,512]{3,2,1,0:T(8,128)(2,1)S(1)}, u32[]{:S(2)}, u32[]{:S(2)}) collective-permute-start(bf16[2,4,16,512]{3,2,1,0:T(8,128)(2,1)S(1)} %slice.55), channel_id=1, source_target_pairs={{0,8},{1,9},{2,10},{3,11},{4,12},{5,13},{6,14},{7,15},{8,16},{9,17... | collective-permute-start | bytes 393224 | tf_op jit(solution)/shard_map/ppermute | solution.py:31
  68.7 3.2 %collective-permute-start.28 = (bf16[2,4,16,512]{3,2,1,0:T(8,128)(2,1)S(1)}, bf16[2,4,16,512]{3,2,1,0:T(8,128)(2,1)S(1)}, u32[]{:S(2)}, u32[]{:S(2)}) collective-permute-start(bf16[2,4,16,512]{3,2,1,0:T(8,128)(2,1)S(1)} %slice.59), channel_id=1, source_target_pairs={{0,3},{1,0},{2,1},{3,2},{4,7},{5,4},{6,5},{7,6},{8,11},{9,8},{10,9... | collective-permute-start | bytes 393224 | tf_op jit(solution)/shard_map/ppermute | solution.py:31
  72.0 0.7 pad_bitcast_fusion.refs_25_
  72.8 1.7 %collective-permute-done.28.refs_19_ = bf16[2,4,16,512]{3,2,1,0:T(8,128)(2,1)S(1)} collective-permute-done((bf16[2,4,16,512]{3,2,1,0:T(8,128)(2,1)S(1)}, bf16[2,4,16,512]{3,2,1,0:T(8,128)(2,1)S(1)}, u32[]{:S(2)}, u32[]{:S(2)}) %collective-permute-start.28) | collective-permute-done | bytes 131104 | tf_op jit(solution)/shard_map/ppermute | solution.py:31
  74.5 3.7 %collective-permute-done.27.refs_18_ = bf16[2,4,16,512]{3,2,1,0:T(8,128)(2,1)S(1)} collective-permute-done((bf16[2,4,16,512]{3,2,1,0:T(8,128)(2,1)S(1)}, bf16[2,4,16,512]{3,2,1,0:T(8,128)(2,1)S(1)}, u32[]{:S(2)}, u32[]{:S(2)}) %collective-permute-start.27) | collective-permute-done | bytes 131104 | tf_op jit(solution)/shard_map/ppermute | solution.py:31
  78.1 1.2 %copy-done = bf16[1,512,1024]{2,1,0:T(8,128)(2,1)S(1)} copy-done((bf16[1,512,1024]{2,1,0:T(8,128)(2,1)S(1)}, bf16[1,512,1024]{2,1,0:T(8,128)(2,1)}, u32[]{:S(2)}) %copy-start) | copy-done | bytes 1048600
  79.4 0.7 copy-done.1
  80.7 9.1 %shard_map.82 = f32[1,512,1024]{2,1,0:T(8,128)} custom-call(s32[3]{0:T(128)S(1)} %pad_add_fusion.place_ref, bf16[4,4,16,512]{3,2,1,0:T(8,128)(2,1)S(1)} %pad_maximum_fusion.refs_0_, bf16[4,4,16,512]{3,2,1,0:T(8,128)(2,1)S(1)} %collective-permute-done.3.refs_1_, bf16[4,4,16,512]{3,2,1,0:T(8,128)(2,1)S(1)} %collective-permute-done.4.refs_2_, ...), custom_call_target="tpu_custom_call" | custom-call | tf_op jit(solution)/shard_map/pallas_call | solution.py:126
  (54 shorter events, 4.3 us)
Async XLA Ops:
  14.1 11.7 %collective-permute-start.14 = (bf16[8,16,512]{2,1,0:T(8,128)(2,1)S(1)}, bf16[8,16,512]{2,1,0:T(8,128)(2,1)S(1)}, u32[]{:S(2)}, u32[]{:S(2)}) collective-permute-start(bf16[8,16,512]{2,1,0:T(8,128)(2,1)S(1)} %all_to_all.5), channel_id=1, source_target_pairs={{0,4},{1,5},{2,6},{3,7},{4,0},{5,1},{6,2},{7,3},{8,12},{9,13},{10,... | collective-permute-start | bytes 393224 | tf_op jit(solution)/shard_map/ppermute | solution.py:31
  18.7 13.9 %collective-permute-start.8 = (bf16[4,16,512]{2,1,0:T(8,128)(2,1)S(1)}, bf16[4,16,512]{2,1,0:T(8,128)(2,1)S(1)}, u32[]{:S(2)}, u32[]{:S(2)}) collective-permute-start(bf16[4,16,512]{2,1,0:T(8,128)(2,1)S(1)} %get-tuple-element.11), channel_id=1, source_target_pairs={{0,24},{1,25},{2,26},{3,27},{4,28},{5,29},{6,30},{7,31},{8,0},{9,1... | collective-permute-start | bytes 196616 | tf_op jit(solution)/shard_map/ppermute | solution.py:31
  19.5 15.5 %collective-permute-start.7 = (bf16[4,16,512]{2,1,0:T(8,128)(2,1)S(1)}, bf16[4,16,512]{2,1,0:T(8,128)(2,1)S(1)}, u32[]{:S(2)}, u32[]{:S(2)}) collective-permute-start(bf16[4,16,512]{2,1,0:T(8,128)(2,1)S(1)} %get-tuple-element.11), channel_id=1, source_target_pairs={{0,8},{1,9},{2,10},{3,11},{4,12},{5,13},{6,14},{7,15},{8,16},{9,17... | collective-permute-start | bytes 196616 | tf_op jit(solution)/shard_map/ppermute | solution.py:31
  22.0 6.9 %collective-permute-start.1 = (bf16[4,16,512]{2,1,0:T(8,128)(2,1)S(1)}, bf16[4,16,512]{2,1,0:T(8,128)(2,1)S(1)}, u32[]{:S(2)}, u32[]{:S(2)}) collective-permute-start(bf16[4,16,512]{2,1,0:T(8,128)(2,1)S(1)} %get-tuple-element.12), channel_id=1, source_target_pairs={{0,3},{1,0},{2,1},{3,2},{4,7},{5,4},{6,5},{7,6},{8,11},{9,8},{10,9... | collective-permute-start | bytes 196616 | tf_op jit(solution)/shard_map/ppermute | solution.py:31
  24.7 5.5 %collective-permute-start = (bf16[4,16,512]{2,1,0:T(8,128)(2,1)S(1)}, bf16[4,16,512]{2,1,0:T(8,128)(2,1)S(1)}, u32[]{:S(2)}, u32[]{:S(2)}) collective-permute-start(bf16[4,16,512]{2,1,0:T(8,128)(2,1)S(1)} %get-tuple-element.12), channel_id=1, source_target_pairs={{0,1},{1,2},{2,3},{3,0},{4,5},{5,6},{6,7},{7,4},{8,9},{9,10},{10,1... | collective-permute-start | bytes 196616 | tf_op jit(solution)/shard_map/ppermute | solution.py:31
  25.8 5.8 %collective-permute-start.2 = (bf16[4,16,512]{2,1,0:T(8,128)(2,1)S(1)}, bf16[4,16,512]{2,1,0:T(8,128)(2,1)S(1)}, u32[]{:S(2)}, u32[]{:S(2)}) collective-permute-start(bf16[4,16,512]{2,1,0:T(8,128)(2,1)S(1)} %get-tuple-element.12), channel_id=1, source_target_pairs={{0,2},{1,3},{2,0},{3,1},{4,6},{5,7},{6,4},{7,5},{8,10},{9,11},{10,... | collective-permute-start | bytes 196616 | tf_op jit(solution)/shard_map/ppermute | solution.py:31
  28.9 8.8 %collective-permute-start.9 = (bf16[4,16,512]{2,1,0:T(8,128)(2,1)S(1)}, bf16[4,16,512]{2,1,0:T(8,128)(2,1)S(1)}, u32[]{:S(2)}, u32[]{:S(2)}) collective-permute-start(bf16[4,16,512]{2,1,0:T(8,128)(2,1)S(1)} %get-tuple-element.11), channel_id=1, source_target_pairs={{0,16},{1,17},{2,18},{3,19},{4,20},{5,21},{6,22},{7,23},{8,24},{9,... | collective-permute-start | bytes 196616 | tf_op jit(solution)/shard_map/ppermute | solution.py:31
  30.2 7.5 %collective-permute-start.23 = (bf16[4,16,512]{2,1,0:T(8,128)(2,1)S(1)}, bf16[4,16,512]{2,1,0:T(8,128)(2,1)S(1)}, u32[]{:S(2)}, u32[]{:S(2)}) collective-permute-start(bf16[4,16,512]{2,1,0:T(8,128)(2,1)S(1)} %get-tuple-element.7), channel_id=1, source_target_pairs={{0,24},{1,25},{2,26},{3,27},{4,28},{5,29},{6,30},{7,31},{8,0},{9,1... | collective-permute-start | bytes 196616 | tf_op jit(solution)/shard_map/ppermute | solution.py:31
  31.6 20.1 %collective-permute-start.4 = (bf16[4,4,16,512]{3,2,1,0:T(8,128)(2,1)S(1)}, bf16[4,4,16,512]{3,2,1,0:T(8,128)(2,1)S(1)}, u32[]{:S(2)}, u32[]{:S(2)}) collective-permute-start(bf16[4,4,16,512]{3,2,1,0:T(8,128)(2,1)S(1)} %pad_maximum_fusion.refs_0_), channel_id=1, source_target_pairs={{0,24},{1,25},{2,26},{3,27},{4,28},{5,29},{6,30},{7,31},{8,0},{9,1... | collective-permute-start | bytes 786440 | tf_op jit(solution)/shard_map/ppermute | solution.py:31
  32.6 21.2 %collective-permute-start.3 = (bf16[4,4,16,512]{3,2,1,0:T(8,128)(2,1)S(1)}, bf16[4,4,16,512]{3,2,1,0:T(8,128)(2,1)S(1)}, u32[]{:S(2)}, u32[]{:S(2)}) collective-permute-start(bf16[4,4,16,512]{3,2,1,0:T(8,128)(2,1)S(1)} %pad_maximum_fusion.refs_0_), channel_id=1, source_target_pairs={{0,8},{1,9},{2,10},{3,11},{4,12},{5,13},{6,14},{7,15},{8,16},{9,17... | collective-permute-start | bytes 786440 | tf_op jit(solution)/shard_map/ppermute | solution.py:31
  35.0 5.2 %collective-permute-start.16 = (bf16[4,16,512]{2,1,0:T(8,128)(2,1)S(1)}, bf16[4,16,512]{2,1,0:T(8,128)(2,1)S(1)}, u32[]{:S(2)}, u32[]{:S(2)}) collective-permute-start(bf16[4,16,512]{2,1,0:T(8,128)(2,1)S(1)} %get-tuple-element.8), channel_id=1, source_target_pairs={{0,3},{1,0},{2,1},{3,2},{4,7},{5,4},{6,5},{7,6},{8,11},{9,8},{10,9... | collective-permute-start | bytes 196616 | tf_op jit(solution)/shard_map/ppermute | solution.py:31
  37.7 6.2 %collective-permute-start.15 = (bf16[4,16,512]{2,1,0:T(8,128)(2,1)S(1)}, bf16[4,16,512]{2,1,0:T(8,128)(2,1)S(1)}, u32[]{:S(2)}, u32[]{:S(2)}) collective-permute-start(bf16[4,16,512]{2,1,0:T(8,128)(2,1)S(1)} %get-tuple-element.8), channel_id=1, source_target_pairs={{0,1},{1,2},{2,3},{3,0},{4,5},{5,6},{6,7},{7,4},{8,9},{9,10},{10,1... | collective-permute-start | bytes 196616 | tf_op jit(solution)/shard_map/ppermute | solution.py:31
  37.7 6.3 %collective-permute-start.17 = (bf16[4,16,512]{2,1,0:T(8,128)(2,1)S(1)}, bf16[4,16,512]{2,1,0:T(8,128)(2,1)S(1)}, u32[]{:S(2)}, u32[]{:S(2)}) collective-permute-start(bf16[4,16,512]{2,1,0:T(8,128)(2,1)S(1)} %get-tuple-element.8), channel_id=1, source_target_pairs={{0,2},{1,3},{2,0},{3,1},{4,6},{5,7},{6,4},{7,5},{8,10},{9,11},{10,... | collective-permute-start | bytes 196616 | tf_op jit(solution)/shard_map/ppermute | solution.py:31
  40.2 15.8 %collective-permute-start.11 = (bf16[4,4,16,512]{3,2,1,0:T(8,128)(2,1)S(1)}, bf16[4,4,16,512]{3,2,1,0:T(8,128)(2,1)S(1)}, u32[]{:S(2)}, u32[]{:S(2)}) collective-permute-start(bf16[4,4,16,512]{3,2,1,0:T(8,128)(2,1)S(1)} %pad_maximum_fusion.1.refs_5_), channel_id=1, source_target_pairs={{0,3},{1,0},{2,1},{3,2},{4,7},{5,4},{6,5},{7,6},{8,11},{9,8},{10,9... | collective-permute-start | bytes 786440 | tf_op jit(solution)/shard_map/ppermute | solution.py:31
  43.9 5.0 %collective-permute-start.22 = (bf16[4,16,512]{2,1,0:T(8,128)(2,1)S(1)}, bf16[4,16,512]{2,1,0:T(8,128)(2,1)S(1)}, u32[]{:S(2)}, u32[]{:S(2)}) collective-permute-start(bf16[4,16,512]{2,1,0:T(8,128)(2,1)S(1)} %get-tuple-element.7), channel_id=1, source_target_pairs={{0,8},{1,9},{2,10},{3,11},{4,12},{5,13},{6,14},{7,15},{8,16},{9,17... | collective-permute-start | bytes 196616 | tf_op jit(solution)/shard_map/ppermute | solution.py:31
  44.0 6.5 %collective-permute-start.24 = (bf16[4,16,512]{2,1,0:T(8,128)(2,1)S(1)}, bf16[4,16,512]{2,1,0:T(8,128)(2,1)S(1)}, u32[]{:S(2)}, u32[]{:S(2)}) collective-permute-start(bf16[4,16,512]{2,1,0:T(8,128)(2,1)S(1)} %get-tuple-element.7), channel_id=1, source_target_pairs={{0,16},{1,17},{2,18},{3,19},{4,20},{5,21},{6,22},{7,23},{8,24},{9,... | collective-permute-start | bytes 196616 | tf_op jit(solution)/shard_map/ppermute | solution.py:31
  48.9 9.1 %collective-permute-start.10 = (bf16[4,4,16,512]{3,2,1,0:T(8,128)(2,1)S(1)}, bf16[4,4,16,512]{3,2,1,0:T(8,128)(2,1)S(1)}, u32[]{:S(2)}, u32[]{:S(2)}) collective-permute-start(bf16[4,4,16,512]{3,2,1,0:T(8,128)(2,1)S(1)} %pad_maximum_fusion.1.refs_5_), channel_id=1, source_target_pairs={{0,1},{1,2},{2,3},{3,0},{4,5},{5,6},{6,7},{7,4},{8,9},{9,10},{10,1... | collective-permute-start | bytes 786440 | tf_op jit(solution)/shard_map/ppermute | solution.py:31
  50.5 7.7 %collective-permute-start.19 = (bf16[4,4,16,512]{3,2,1,0:T(8,128)(2,1)S(1)}, bf16[4,4,16,512]{3,2,1,0:T(8,128)(2,1)S(1)}, u32[]{:S(2)}, u32[]{:S(2)}) collective-permute-start(bf16[4,4,16,512]{3,2,1,0:T(8,128)(2,1)S(1)} %pad_maximum_fusion.2.refs_10_), channel_id=1, source_target_pairs={{0,24},{1,25},{2,26},{3,27},{4,28},{5,29},{6,30},{7,31},{8,0},{9,1... | collective-permute-start | bytes 786440 | tf_op jit(solution)/shard_map/ppermute | solution.py:31
  51.8 9.5 %collective-permute-start.18 = (bf16[4,4,16,512]{3,2,1,0:T(8,128)(2,1)S(1)}, bf16[4,4,16,512]{3,2,1,0:T(8,128)(2,1)S(1)}, u32[]{:S(2)}, u32[]{:S(2)}) collective-permute-start(bf16[4,4,16,512]{3,2,1,0:T(8,128)(2,1)S(1)} %pad_maximum_fusion.2.refs_10_), channel_id=1, source_target_pairs={{0,8},{1,9},{2,10},{3,11},{4,12},{5,13},{6,14},{7,15},{8,16},{9,17... | collective-permute-start | bytes 786440 | tf_op jit(solution)/shard_map/ppermute | solution.py:31
  53.8 11.4 %collective-permute-start.26 = (bf16[4,4,16,512]{3,2,1,0:T(8,128)(2,1)S(1)}, bf16[4,4,16,512]{3,2,1,0:T(8,128)(2,1)S(1)}, u32[]{:S(2)}, u32[]{:S(2)}) collective-permute-start(bf16[4,4,16,512]{3,2,1,0:T(8,128)(2,1)S(1)} %pad_maximum_fusion.3.refs_15_), channel_id=1, source_target_pairs={{0,3},{1,0},{2,1},{3,2},{4,7},{5,4},{6,5},{7,6},{8,11},{9,8},{10,9... | collective-permute-start | bytes 786440 | tf_op jit(solution)/shard_map/ppermute | solution.py:31
  56.0 9.3 %collective-permute-start.25 = (bf16[4,4,16,512]{3,2,1,0:T(8,128)(2,1)S(1)}, bf16[4,4,16,512]{3,2,1,0:T(8,128)(2,1)S(1)}, u32[]{:S(2)}, u32[]{:S(2)}) collective-permute-start(bf16[4,4,16,512]{3,2,1,0:T(8,128)(2,1)S(1)} %pad_maximum_fusion.3.refs_15_), channel_id=1, source_target_pairs={{0,1},{1,2},{2,3},{3,0},{4,5},{5,6},{6,7},{7,4},{8,9},{9,10},{10,1... | collective-permute-start | bytes 786440 | tf_op jit(solution)/shard_map/ppermute | solution.py:31
  58.0 7.5 %collective-permute-start.6 = (bf16[2,4,16,512]{3,2,1,0:T(8,128)(2,1)}, bf16[2,4,16,512]{3,2,1,0:T(8,128)(2,1)S(1)}, u32[]{:S(2)}, u32[]{:S(2)}) collective-permute-start(bf16[2,4,16,512]{3,2,1,0:T(8,128)(2,1)} %slice.50), channel_id=1, source_target_pairs={{0,24},{1,25},{2,26},{3,27},{4,28},{5,29},{6,30},{7,31},{8,0},{9,1... | collective-permute-start | bytes 393224 | tf_op jit(solution)/shard_map/ppermute | solution.py:31
  58.2 10.5 %collective-permute-start.5 = (bf16[2,4,16,512]{3,2,1,0:T(8,128)(2,1)}, bf16[2,4,16,512]{3,2,1,0:T(8,128)(2,1)S(1)}, u32[]{:S(2)}, u32[]{:S(2)}) collective-permute-start(bf16[2,4,16,512]{3,2,1,0:T(8,128)(2,1)} %slice.49), channel_id=1, source_target_pairs={{0,8},{1,9},{2,10},{3,11},{4,12},{5,13},{6,14},{7,15},{8,16},{9,17... | collective-permute-start | bytes 393224 | tf_op jit(solution)/shard_map/ppermute | solution.py:31
  61.2 10.7 %collective-permute-start.13 = (bf16[2,4,16,512]{3,2,1,0:T(8,128)(2,1)}, bf16[2,4,16,512]{3,2,1,0:T(8,128)(2,1)S(1)}, u32[]{:S(2)}, u32[]{:S(2)}) collective-permute-start(bf16[2,4,16,512]{3,2,1,0:T(8,128)(2,1)} %slice.53), channel_id=1, source_target_pairs={{0,3},{1,0},{2,1},{3,2},{4,7},{5,4},{6,5},{7,6},{8,11},{9,8},{10,9... | collective-permute-start | bytes 393224 | tf_op jit(solution)/shard_map/ppermute | solution.py:31
  65.2 7.5 %collective-permute-start.12 = (bf16[2,4,16,512]{3,2,1,0:T(8,128)(2,1)S(1)}, bf16[2,4,16,512]{3,2,1,0:T(8,128)(2,1)S(1)}, u32[]{:S(2)}, u32[]{:S(2)}) collective-permute-start(bf16[2,4,16,512]{3,2,1,0:T(8,128)(2,1)S(1)} %slice.52), channel_id=1, source_target_pairs={{0,1},{1,2},{2,3},{3,0},{4,5},{5,6},{6,7},{7,4},{8,9},{9,10},{10,1... | collective-permute-start | bytes 393224 | tf_op jit(solution)/shard_map/ppermute | solution.py:31
  65.3 7.4 %collective-permute-start.21 = (bf16[2,4,16,512]{3,2,1,0:T(8,128)(2,1)S(1)}, bf16[2,4,16,512]{3,2,1,0:T(8,128)(2,1)S(1)}, u32[]{:S(2)}, u32[]{:S(2)}) collective-permute-start(bf16[2,4,16,512]{3,2,1,0:T(8,128)(2,1)S(1)} %slice.56), channel_id=1, source_target_pairs={{0,24},{1,25},{2,26},{3,27},{4,28},{5,29},{6,30},{7,31},{8,0},{9,1... | collective-permute-start | bytes 393224 | tf_op jit(solution)/shard_map/ppermute | solution.py:31
  65.4 7.3 %collective-permute-start.20 = (bf16[2,4,16,512]{3,2,1,0:T(8,128)(2,1)S(1)}, bf16[2,4,16,512]{3,2,1,0:T(8,128)(2,1)S(1)}, u32[]{:S(2)}, u32[]{:S(2)}) collective-permute-start(bf16[2,4,16,512]{3,2,1,0:T(8,128)(2,1)S(1)} %slice.55), channel_id=1, source_target_pairs={{0,8},{1,9},{2,10},{3,11},{4,12},{5,13},{6,14},{7,15},{8,16},{9,17... | collective-permute-start | bytes 393224 | tf_op jit(solution)/shard_map/ppermute | solution.py:31
  68.7 5.7 %collective-permute-start.28 = (bf16[2,4,16,512]{3,2,1,0:T(8,128)(2,1)S(1)}, bf16[2,4,16,512]{3,2,1,0:T(8,128)(2,1)S(1)}, u32[]{:S(2)}, u32[]{:S(2)}) collective-permute-start(bf16[2,4,16,512]{3,2,1,0:T(8,128)(2,1)S(1)} %slice.59), channel_id=1, source_target_pairs={{0,3},{1,0},{2,1},{3,2},{4,7},{5,4},{6,5},{7,6},{8,11},{9,8},{10,9... | collective-permute-start | bytes 393224 | tf_op jit(solution)/shard_map/ppermute | solution.py:31
  72.0 6.2 %collective-permute-start.27 = (bf16[2,4,16,512]{3,2,1,0:T(8,128)(2,1)S(1)}, bf16[2,4,16,512]{3,2,1,0:T(8,128)(2,1)S(1)}, u32[]{:S(2)}, u32[]{:S(2)}) collective-permute-start(bf16[2,4,16,512]{3,2,1,0:T(8,128)(2,1)S(1)} %slice.58), channel_id=1, source_target_pairs={{0,1},{1,2},{2,3},{3,0},{4,5},{5,6},{6,7},{7,4},{8,9},{9,10},{10,1... | collective-permute-start | bytes 393224 | tf_op jit(solution)/shard_map/ppermute | solution.py:31
  78.1 1.2 %copy-start = (bf16[1,512,1024]{2,1,0:T(8,128)(2,1)S(1)}, bf16[1,512,1024]{2,1,0:T(8,128)(2,1)}, u32[]{:S(2)}) copy-start(bf16[1,512,1024]{2,1,0:T(8,128)(2,1)} %refs_21_.1) | copy-start | bytes 3145732
  79.4 0.7 copy-start.1
  80.1 0.7 copy-start.2

commit v2 on v0

v2 whole, which is shorter than its diff:
```python
import functools

import jax
import jax.numpy as jnp
from jax import lax
from jax.experimental import pallas as pl
from jax.experimental.pallas import tpu as pltpu
from jax.sharding import Mesh, PartitionSpec as P

ROW, COL = ("zlo", "core"), ("y", "zhi", "x")
TILE = 256
TILES = 1024 // TILE
NEAR = (0, 3, 1, 2)


def send(block, axis, shift):
    return lax.ppermute(block, axis, [(i, (i + shift) % 4) for i in range(4)])


def near(block, axis):
    back = send(block, axis, 1)
    ahead = send(block, axis, -1)
    far = send(block, axis, 2)
    return jnp.stack([block, back, ahead, far])


def live_kernel(counts_ref, amplitudes_ref, keep_ref, pass_ref):
    core = lax.axis_index("core")
    width = amplitudes_ref.shape[2]
    first = (lax.axis_index("zlo") * 2 + core) * width
    position = first + lax.broadcasted_iota(jnp.int32, (16, width), 1)
    for z in range(4):
        for out_ref, irrep in ((keep_ref, z * 2 + core), (pass_ref, z * 2 + 1 - core)):
            block = amplitudes_ref[irrep]
            out_ref[z] = jnp.where(position < counts_ref[irrep], block, jnp.zeros_like(block))


def pick(table_ref, index):
    high, low = index >> 7, index & 127
    got = jnp.zeros((8, 128), jnp.float32)
    for r in range(table_ref.shape[0]):
        row = jnp.broadcast_to(table_ref[r : r + 1, :], (8, 128))
        got = jnp.where(high == r, jnp.take_along_axis(row, low, axis=1), got)
    return got


def groups_of(pieces):
    out = []
    for number, (half, distance, slots) in enumerate(pieces):
        for k, slot in enumerate(slots):
            dy, dx = (distance, NEAR[slot]) if half == 0 else (NEAR[slot], distance)
            out.append((number, k, half, dy, dx))
    return out


OWN = groups_of([(h, 0, (0, 1, 2, 3)) for h in (0, 1)])
BESIDE = groups_of([(h, d, (0, 1, 2, 3)) for h in (0, 1) for d in (3, 1)])
FAR = groups_of([(h, 2, s) for h in (0, 1) for s in ((0, 1), (2, 3))])


def rows_of(half, dy, dx):
    y, x, z = lax.axis_index("y"), lax.axis_index("x"), lax.axis_index("zhi")
    return pl.ds(pl.multiple_of((((y + dy) % 4 * 2 + (z + half) % 2) * 4 + (x + dx) % 4) * 16, 16), 16)


def update(groups, refs, held_ref, bare_ref, occ_sum_ref, vir_sum_ref, out_ref, live_ref, stage_ref, sem, ready=None):
    core = lax.axis_index("core")
    for g, (number, k, _, _, _) in enumerate(groups):
        for z in range(4):
            for c in range(2):
                panel = pl.multiple_of((z * 2 + (core + c) % 2) * 512, 512)
                live_ref[g * 16 : (g + 1) * 16, pl.ds(panel, 512)] = refs[number][k, z, c]
    copies = []
    for n in range(TILES):
        tile = slice(n * TILE, (n + 1) * TILE)
        if ready is not None:
            ready(n)
        ladder = jnp.dot(live_ref[...], held_ref[:, tile], preferred_element_type=jnp.float32)
        for g, (_, _, half, dy, dx) in enumerate(groups):
            rows = rows_of(half, dy, dx)
            for s in range(TILE // 128):
                cols = slice(n * TILE + s * 128, n * TILE + (s + 1) * 128)
                part = ladder[g * 16 : (g + 1) * 16, s * 128 : (s + 1) * 128]
                residual = bare_ref[0, rows, cols].astype(jnp.float32) + 0.5 * part
                stage_ref[g * 16 : (g + 1) * 16, cols] = residual / (vir_sum_ref[:1, cols] - occ_sum_ref[rows, :])
        for g, (_, _, half, dy, dx) in enumerate(groups):
            copy = pltpu.make_async_copy(
                stage_ref.at[pl.ds(g * 16, 16), pl.ds(n * TILE, TILE)],
                out_ref.at[0, rows_of(half, dy, dx), pl.ds(n * TILE, TILE)],
                sem.at[n, g],
            )
            copy.start()
            copies.append(copy)
    for copy in copies:
        copy.wait()


def own_kernel(*refs):
    (integrals_ref, bare_ref, ij_ref, ab_ref, occ_ref, vir_ref) = refs[2:8]
    (out_ref, held_ref, occ_sum_ref, vir_sum_ref, live_ref, stage_ref, sem, load_sem) = refs[8:]
    loads = []
    for n in range(TILES):
        tile = pl.ds(n * TILE, TILE)
        loads.append(pltpu.make_async_copy(integrals_ref.at[0, :, tile], held_ref.at[:, tile], load_sem.at[n]))
        loads[-1].start()
    for s in range(4):
        cols = slice(s * 128, (s + 1) * 128)
        occ = jnp.zeros((8, 128), jnp.float32)
        for side in range(2):
            occ = occ + pick(occ_ref, jnp.broadcast_to(ij_ref[0, side : side + 1, cols], (8, 128)))
        occ_sum_ref[cols, :] = jnp.broadcast_to(occ[:1], (128, 128)).T
    for s in range(8):
        cols = slice(s * 128, (s + 1) * 128)
        vir = jnp.zeros((8, 128), jnp.float32)
        for side in range(2):
            vir = vir + pick(vir_ref, jnp.broadcast_to(ab_ref[0, side : side + 1, cols], (8, 128)))
        vir_sum_ref[:, cols] = vir
    update(
        OWN, refs[:2], held_ref, bare_ref, occ_sum_ref, vir_sum_ref, out_ref, live_ref, stage_ref, sem,
        ready=lambda n: loads[n].wait(),
    )


def more_kernel(groups, *refs):
    count = len(refs) - 9
    held_ref, bare_ref, occ_sum_ref, vir_sum_ref, _, out_ref, live_ref, stage_ref, sem = refs[count:]
    update(groups, refs[:count], held_ref, bare_ref, occ_sum_ref, vir_sum_ref, out_ref, live_ref, stage_ref, sem)


IN_VMEM = pl.BlockSpec(memory_space=pltpu.VMEM)
IN_HBM = pl.BlockSpec(memory_space=pl.ANY)
PARAMS = pltpu.CompilerParams(vmem_limit_bytes=16 * 1024 * 1024)
RESULT = jax.ShapeDtypeStruct((1, 512, 1024), jnp.float32)


def in_vmem(array):
    return pltpu.with_memory_space_constraint(array, pltpu.VMEM)


def scratch(groups):
    rows = len(groups) * 16
    return [
        pltpu.VMEM((rows, 4096), jnp.bfloat16),
        pltpu.VMEM((rows, 1024), jnp.float32),
        pltpu.SemaphoreType.DMA((TILES, len(groups))),
    ]


def more(groups, pieces, held, bare, occ_sum, vir_sum, begun):
    count = len(pieces) + 4
    return pl.pallas_call(
        functools.partial(more_kernel, groups),
        in_specs=[IN_VMEM] * count + [IN_HBM],
        out_specs=IN_HBM,
        out_shape=RESULT,
        scratch_shapes=scratch(groups),
        input_output_aliases={count: 0},
        compiler_params=PARAMS,
    )(*[in_vmem(p) for p in pieces], held, bare, occ_sum, vir_sum, begun)


def on_device(
    amplitudes, integrals, bare, cd_count, ij_orbitals, ab_orbitals, occ_energy, vir_energy
):
    width = amplitudes.shape[2]
    piece = pltpu.VMEM((4, 16, width), amplitudes.dtype)
    kept, passed = pl.pallas_call(
        live_kernel,
        out_shape=(piece, piece),
        in_specs=[pl.BlockSpec(memory_space=pltpu.SMEM), IN_VMEM],
        out_specs=(IN_VMEM, IN_VMEM),
    )(cd_count, amplitudes)
    given = lax.ppermute(passed, "core", [(0, 1), (1, 0)])
    own = lax.all_to_all(
        jnp.stack([kept, given], axis=1), "zlo", split_axis=0, concat_axis=0, tiled=True
    )
    other = lax.ppermute(own, "zhi", [(0, 1), (1, 0)])
    stacks, beside, far = [], [], []
    for block, one, two in ((own, "x", "y"), (other, "y", "x")):
        blocks = near(block, one)
        back = send(blocks, two, 1)
        ahead = send(blocks, two, -1)
        stacks.append(blocks)
        beside += [back, ahead]
        far += [send(back[:2], two, 1), send(ahead[2:], two, -1)]

    occ_table = jnp.pad(occ_energy, (0, 56)).reshape(2, 128)
    vir_table = jnp.pad(vir_energy, (0, 120)).reshape(15, 128)
    bare = in_vmem(bare)
    begun, held, occ_sum, vir_sum = pl.pallas_call(
        own_kernel,
        in_specs=[IN_VMEM] * 2 + [IN_HBM] + [IN_VMEM] * 5,
        out_specs=[IN_HBM, IN_VMEM, IN_VMEM, IN_VMEM],
        out_shape=(
            RESULT,
            pltpu.VMEM((4096, 1024), jnp.bfloat16),
            pltpu.VMEM((512, 128), jnp.float32),
            pltpu.VMEM((8, 1024), jnp.float32),
        ),
        scratch_shapes=scratch(OWN) + [pltpu.SemaphoreType.DMA((TILES,))],
        compiler_params=PARAMS,
    )(
        *[in_vmem(p) for p in stacks],
        pltpu.with_memory_space_constraint(integrals, pltpu.HBM),
        bare, ij_orbitals, ab_orbitals, occ_table, vir_table,
    )
    begun = more(BESIDE, beside, held, bare, occ_sum, vir_sum, begun)
    return more(FAR, far, held, bare, occ_sum, vir_sum, begun)


def solution(mesh):
    split = Mesh(mesh.devices.reshape(4, 2, 4, 2, 4), ("zlo", "core", "y", "zhi", "x"))
    return jax.shard_map(
        on_device,
        mesh=split,
        in_specs=(
            P(None, COL, ROW),
            P(ROW, None, COL),
            P(ROW, None, COL),
            P(),
            P(ROW, None, None),
            P(ROW, None, COL),
            P(),
            P(),
        ),
        out_specs=P(ROW, None, COL),
        check_vma=False,
    )
```

time: 252 us -> 64.3 us (0.26); the launches traced: 249 us -> 64.2 us
  waiting for transfers between devices: 189 us -> 13.6 us
  local copies, waits for them, and re-layouts: 29.1 us -> 0.11 us
  starting transfers between devices: 4.69 us -> 25.1 us
  between operations: 13.6 us -> 0.34 us
  Pallas kernels: 0 us -> 13 us
  blocking collectives: 0 us -> 11.9 us
  matrix products: 9.43 us -> 0 us
  other arithmetic: 3.32 us -> 0.15 us
    all_gather x1 -> x0, waiting for transfers between devices: 116 us -> none  [on_device(): gathered = lax.all_gather(amplitudes, 'col', axis=1, tiled=True)]
    all_to_all x1 -> x0, waiting for transfers between devices: 73.2 us -> none  [on_device(): lax.all_to_all(gathered, 'row', split_axis=0, concat_axis=2, tiled=True)]
    ppermute x0 -> x16, starting transfers between devices: none -> 25.1 us  [the longest x14 20.5 us: send(): return lax.ppermute(block, axis, [(i, (i + shift) % 4) for i in range(4)])]
    gather x4 -> x0, local copies, waits for them, and re-layouts: 19.3 us -> none  [the longest x1 6.15 us: on_device(): jnp.take(vir_energy, ab_orbitals[:, 0, :])]
    ppermute x0 -> x16, waiting for transfers between devices: none -> 13.6 us  [the longest x14 11.3 us: send(): return lax.ppermute(block, axis, [(i, (i + shift) % 4) for i in range(4)])]
    pallas_call x0 -> x4, Pallas kernels: none -> 13 us  [the longest x2 6.22 us: more(): pl.pallas_call(functools.partial(more_kernel, groups), in_specs=[IN_VMEM]...]
    all_to_all x0 -> x1, blocking collectives: none -> 11.9 us  [on_device(): lax.all_to_all(jnp.stack([kept, given], axis=1), 'zlo', split_axis=0, con...]
    dot_general x1 -> x0, matrix products: 9.43 us -> none  [on_device(): jnp.einsum('hic,hca->hia', jnp.where(positions[None, None, :] < counts[:,...]
  transfers between devices with their start and end apart: 2 -> 16, of which waited for: 2 -> 6; matrix products, arithmetic and copies ran while one was open for 8% -> 0% of each run, Pallas kernels for 0% -> 15%
where the time goes in v2:
time: 64.3 us; the launch traced here: 64.2 us
  starting transfers between devices  25.1 us (39%)
  waiting for transfers between devices  13.6 us (21%)
  Pallas kernels  13 us (20%)
  blocking collectives  11.9 us (19%)
    ppermute x14, starting transfers between devices, send(): return lax.ppermute(block, axis, [(i, (i + shift) % 4) for i in range(4)])  20.5 us
    all_to_all x1, blocking collectives, on_device(): lax.all_to_all(jnp.stack([kept, given], axis=1), 'zlo', split_axis=0, con...  11.9 us
    ppermute x14, waiting for transfers between devices, send(): return lax.ppermute(block, axis, [(i, (i + shift) % 4) for i in range(4)])  11.3 us
    pallas_call x2, Pallas kernels, more(): pl.pallas_call(functools.partial(more_kernel, groups), in_specs=[IN_VMEM]...  6.22 us
    pallas_call x1, Pallas kernels, on_device(): pl.pallas_call(own_kernel, in_specs=[IN_VMEM] * 2 + [IN_HBM] + [IN_VMEM]...  5.8 us
    ppermute x1, starting transfers between devices, on_device(): other = lax.ppermute(own, 'zhi', [(0, 1), (1, 0)])  4.49 us
  transfers between devices with their start and end apart: 16, of which 6 were waited for; matrix products, arithmetic and copies ran while one was open for 0% of the time, Pallas kernels for 15%

profile of v2, /device:TPU:8, one launch (start us, length us, event | category | flops | bytes accessed | tf_op | source)
XLA Modules:
  0.0 64.2 jit_solution(17156711336769101631)
XLA Ops:
  0.0 0.9 %shard_map.82 = (bf16[4,16,512]{2,1,0:T(8,128)(2,1)S(1)}, bf16[4,16,512]{2,1,0:T(8,128)(2,1)S(1)}) custom-call(s32[8]{0:T(128)} %counts_ref.1, bf16[8,16,512]{2,1,0:T(8,128)(2,1)} %amplitudes_ref.1), custom_call_target="tpu_custom_call" | custom-call | tf_op jit(solution)/shard_map/pallas_call | solution.py:167
  0.9 0.1 collective-permute-start
  1.0 1.2 %collective-permute-done = bf16[4,16,512]{2,1,0:T(8,128)(2,1)S(1)} collective-permute-done((bf16[4,16,512]{2,1,0:T(8,128)(2,1)S(1)}, bf16[4,16,512]{2,1,0:T(8,128)(2,1)S(1)}, u32[]{:S(2)}, u32[]{:S(2)}) %collective-permute-start) | collective-permute-done | bytes 65568 | tf_op jit(solution)/shard_map/ppermute | solution.py:173
  2.3 11.9 %all_to_all.5 = bf16[4,2,16,512]{3,2,1,0:T(8,128)(2,1)S(1)} all-to-all(bf16[4,2,16,512]{3,2,1,0:T(8,128)(2,1)S(1)} %pad_maximum_fusion.2), channel_id=1, replica_groups=mesh['zlo'=4,'core'=2,'y'=4,'zhi'=2,'x'=4] {'zlo'}, dimensions={0} | all-to-all | bytes 262144 | tf_op jit(solution)/shard_map/all_to_all | solution.py:174
  14.2 4.5 %collective-permute-start.8 = (bf16[4,2,16,512]{3,2,1,0:T(8,128)(2,1)S(1)}, bf16[4,2,16,512]{3,2,1,0:T(8,128)(2,1)S(1)}, u32[]{:S(2)}, u32[]{:S(2)}) collective-permute-start(bf16[4,2,16,512]{3,2,1,0:T(8,128)(2,1)S(1)} %all_to_all.5), channel_id=1, source_target_pairs={{0,4},{4,0},{1,5},{5,1},{2,6},{6,2},{3,7},{7,3},{8,12},{12,8},{9,1... | collective-permute-start | bytes 393224 | tf_op jit(solution)/shard_map/ppermute | solution.py:177
  18.7 1.5 %collective-permute-start.1 = (bf16[4,2,16,512]{3,2,1,0:T(8,128)(2,1)S(1)}, bf16[4,2,16,512]{3,2,1,0:T(8,128)(2,1)S(1)}, u32[]{:S(2)}, u32[]{:S(2)}) collective-permute-start(bf16[4,2,16,512]{3,2,1,0:T(8,128)(2,1)S(1)} %all_to_all.5), channel_id=1, source_target_pairs={{0,1},{1,2},{2,3},{3,0},{4,5},{5,6},{6,7},{7,4},{8,9},{9,10},{10,1... | collective-permute-start | bytes 393224 | tf_op jit(solution)/shard_map/ppermute | solution.py:17
  20.2 1.7 %collective-permute-start.2 = (bf16[4,2,16,512]{3,2,1,0:T(8,128)(2,1)S(1)}, bf16[4,2,16,512]{3,2,1,0:T(8,128)(2,1)S(1)}, u32[]{:S(2)}, u32[]{:S(2)}) collective-permute-start(bf16[4,2,16,512]{3,2,1,0:T(8,128)(2,1)S(1)} %all_to_all.5), channel_id=1, source_target_pairs={{0,3},{1,0},{2,1},{3,2},{4,7},{5,4},{6,5},{7,6},{8,11},{9,8},{10,9... | collective-permute-start | bytes 393224 | tf_op jit(solution)/shard_map/ppermute | solution.py:17
  22.0 1.8 %collective-permute-start.3 = (bf16[4,2,16,512]{3,2,1,0:T(8,128)(2,1)S(1)}, bf16[4,2,16,512]{3,2,1,0:T(8,128)(2,1)S(1)}, u32[]{:S(2)}, u32[]{:S(2)}) collective-permute-start(bf16[4,2,16,512]{3,2,1,0:T(8,128)(2,1)S(1)} %all_to_all.5), channel_id=1, source_target_pairs={{0,2},{1,3},{2,0},{3,1},{4,6},{5,7},{6,4},{7,5},{8,10},{9,11},{10,... | collective-permute-start | bytes 393224 | tf_op jit(solution)/shard_map/ppermute | solution.py:17
  23.8 1.1 %collective-permute-done.8 = bf16[4,2,16,512]{3,2,1,0:T(8,128)(2,1)S(1)} collective-permute-done((bf16[4,2,16,512]{3,2,1,0:T(8,128)(2,1)S(1)}, bf16[4,2,16,512]{3,2,1,0:T(8,128)(2,1)S(1)}, u32[]{:S(2)}, u32[]{:S(2)}) %collective-permute-start.8) | collective-permute-done | bytes 131104 | tf_op jit(solution)/shard_map/ppermute | solution.py:177
  24.9 1.6 %collective-permute-start.9 = (bf16[4,2,16,512]{3,2,1,0:T(8,128)(2,1)S(1)}, bf16[4,2,16,512]{3,2,1,0:T(8,128)(2,1)S(1)}, u32[]{:S(2)}, u32[]{:S(2)}) collective-permute-start(bf16[4,2,16,512]{3,2,1,0:T(8,128)(2,1)S(1)} %collective-permute-done.8), channel_id=1, source_target_pairs={{0,8},{8,16},{16,24},{24,0},{1,9},{9,17},{17,25},{25,1},{2,10},{10... | collective-permute-start | bytes 393224 | tf_op jit(solution)/shard_map/ppermute | solution.py:17
  26.5 0.4 collective-permute-start.10
  26.9 2.3 %collective-permute-start.11 = (bf16[4,2,16,512]{3,2,1,0:T(8,128)(2,1)S(1)}, bf16[4,2,16,512]{3,2,1,0:T(8,128)(2,1)S(1)}, u32[]{:S(2)}, u32[]{:S(2)}) collective-permute-start(bf16[4,2,16,512]{3,2,1,0:T(8,128)(2,1)S(1)} %collective-permute-done.8), channel_id=1, source_target_pairs={{0,16},{8,24},{16,0},{24,8},{1,17},{9,25},{17,1},{25,9},{2,18},{10... | collective-permute-start | bytes 393224 | tf_op jit(solution)/shard_map/ppermute | solution.py:17
  29.2 0.0 copy-start.3
  29.2 0.0 copy-start
  29.3 0.0 copy-start.2
  29.3 0.1 pad_maximum_fusion.refs_0_
  29.3 0.9 %collective-permute-start.4 = (bf16[4,4,2,16,512]{4,3,2,1,0:T(8,128)(2,1)S(1)}, bf16[4,4,2,16,512]{4,3,2,1,0:T(8,128)(2,1)S(1)}, u32[]{:S(2)}, u32[]{:S(2)}) collective-permute-start(bf16[4,4,2,16,512]{4,3,2,1,0:T(8,128)(2,1)S(1)} %pad_maximum_fusion.refs_0_), channel_id=1, source_target_pairs={{0,8},{8,16},{16,24},{24,0},{1,9},{9,17},{17,25},{25,1},{2,10},{10... | collective-permute-start | bytes 1572872 | tf_op jit(solution)/shard_map/ppermute | solution.py:17
  30.3 1.2 %collective-permute-start.6 = (bf16[4,4,2,16,512]{4,3,2,1,0:T(8,128)(2,1)S(1)}, bf16[4,4,2,16,512]{4,3,2,1,0:T(8,128)(2,1)S(1)}, u32[]{:S(2)}, u32[]{:S(2)}) collective-permute-start(bf16[4,4,2,16,512]{4,3,2,1,0:T(8,128)(2,1)S(1)} %pad_maximum_fusion.refs_0_), channel_id=1, source_target_pairs={{0,24},{8,0},{16,8},{24,16},{1,25},{9,1},{17,9},{25,17},{2,26},{10... | collective-permute-start | bytes 1572872 | tf_op jit(solution)/shard_map/ppermute | solution.py:17
  31.5 1.3 %collective-permute-done.10 = bf16[4,2,16,512]{3,2,1,0:T(8,128)(2,1)S(1)} collective-permute-done((bf16[4,2,16,512]{3,2,1,0:T(8,128)(2,1)S(1)}, bf16[4,2,16,512]{3,2,1,0:T(8,128)(2,1)S(1)}, u32[]{:S(2)}, u32[]{:S(2)}) %collective-permute-start.10) | collective-permute-done | bytes 131104 | tf_op jit(solution)/shard_map/ppermute | solution.py:17
  32.8 3.5 %collective-permute-done.11 = bf16[4,2,16,512]{3,2,1,0:T(8,128)(2,1)S(1)} collective-permute-done((bf16[4,2,16,512]{3,2,1,0:T(8,128)(2,1)S(1)}, bf16[4,2,16,512]{3,2,1,0:T(8,128)(2,1)S(1)}, u32[]{:S(2)}, u32[]{:S(2)}) %collective-permute-start.11) | collective-permute-done | bytes 131104 | tf_op jit(solution)/shard_map/ppermute | solution.py:17
  36.3 0.1 pad_maximum_fusion.1.refs_1_
  36.4 1.7 %collective-permute-start.12 = (bf16[4,4,2,16,512]{4,3,2,1,0:T(8,128)(2,1)S(1)}, bf16[4,4,2,16,512]{4,3,2,1,0:T(8,128)(2,1)S(1)}, u32[]{:S(2)}, u32[]{:S(2)}) collective-permute-start(bf16[4,4,2,16,512]{4,3,2,1,0:T(8,128)(2,1)S(1)} %pad_maximum_fusion.1.refs_1_), channel_id=1, source_target_pairs={{0,1},{1,2},{2,3},{3,0},{4,5},{5,6},{6,7},{7,4},{8,9},{9,10},{10,1... | collective-permute-start | bytes 1572872 | tf_op jit(solution)/shard_map/ppermute | solution.py:17
  38.1 1.6 %collective-permute-start.14 = (bf16[4,4,2,16,512]{4,3,2,1,0:T(8,128)(2,1)S(1)}, bf16[4,4,2,16,512]{4,3,2,1,0:T(8,128)(2,1)S(1)}, u32[]{:S(2)}, u32[]{:S(2)}) collective-permute-start(bf16[4,4,2,16,512]{4,3,2,1,0:T(8,128)(2,1)S(1)} %pad_maximum_fusion.1.refs_1_), channel_id=1, source_target_pairs={{0,3},{1,0},{2,1},{3,2},{4,7},{5,4},{6,5},{7,6},{8,11},{9,8},{10,9... | collective-permute-start | bytes 1572872 | tf_op jit(solution)/shard_map/ppermute | solution.py:17
  39.7 3.2 %collective-permute-done.4.refs_0_ = bf16[4,4,2,16,512]{4,3,2,1,0:T(8,128)(2,1)S(1)} collective-permute-done((bf16[4,4,2,16,512]{4,3,2,1,0:T(8,128)(2,1)S(1)}, bf16[4,4,2,16,512]{4,3,2,1,0:T(8,128)(2,1)S(1)}, u32[]{:S(2)}, u32[]{:S(2)}) %collective-permute-start.4) | collective-permute-done | bytes 524320 | tf_op jit(solution)/shard_map/ppermute | solution.py:17
  42.9 1.1 %collective-permute-start.5 = (bf16[2,4,2,16,512]{4,3,2,1,0:T(8,128)(2,1)S(1)}, bf16[2,4,2,16,512]{4,3,2,1,0:T(8,128)(2,1)S(1)}, u32[]{:S(2)}, u32[]{:S(2)}) collective-permute-start(bf16[2,4,2,16,512]{4,3,2,1,0:T(8,128)(2,1)S(1)} %slice.16), channel_id=1, source_target_pairs={{0,8},{8,16},{16,24},{24,0},{1,9},{9,17},{17,25},{25,1},{2,10},{10... | collective-permute-start | bytes 786440 | tf_op jit(solution)/shard_map/ppermute | solution.py:17
  44.0 1.1 %collective-permute-start.7 = (bf16[2,4,2,16,512]{4,3,2,1,0:T(8,128)(2,1)S(1)}, bf16[2,4,2,16,512]{4,3,2,1,0:T(8,128)(2,1)S(1)}, u32[]{:S(2)}, u32[]{:S(2)}) collective-permute-start(bf16[2,4,2,16,512]{4,3,2,1,0:T(8,128)(2,1)S(1)} %slice.17), channel_id=1, source_target_pairs={{0,24},{8,0},{16,8},{24,16},{1,25},{9,1},{17,9},{25,17},{2,26},{10... | collective-permute-start | bytes 786440 | tf_op jit(solution)/shard_map/ppermute | solution.py:17
  45.1 3.2 %collective-permute-done.12.refs_2_ = bf16[4,4,2,16,512]{4,3,2,1,0:T(8,128)(2,1)S(1)} collective-permute-done((bf16[4,4,2,16,512]{4,3,2,1,0:T(8,128)(2,1)S(1)}, bf16[4,4,2,16,512]{4,3,2,1,0:T(8,128)(2,1)S(1)}, u32[]{:S(2)}, u32[]{:S(2)}) %collective-permute-start.12) | collective-permute-done | bytes 524320 | tf_op jit(solution)/shard_map/ppermute | solution.py:17
  48.3 1.8 %collective-permute-start.13 = (bf16[2,4,2,16,512]{4,3,2,1,0:T(8,128)(2,1)S(1)}, bf16[2,4,2,16,512]{4,3,2,1,0:T(8,128)(2,1)S(1)}, u32[]{:S(2)}, u32[]{:S(2)}) collective-permute-start(bf16[2,4,2,16,512]{4,3,2,1,0:T(8,128)(2,1)S(1)} %slice.18), channel_id=1, source_target_pairs={{0,1},{1,2},{2,3},{3,0},{4,5},{5,6},{6,7},{7,4},{8,9},{9,10},{10,1... | collective-permute-start | bytes 786440 | tf_op jit(solution)/shard_map/ppermute | solution.py:17
  50.2 1.8 %collective-permute-start.15 = (bf16[2,4,2,16,512]{4,3,2,1,0:T(8,128)(2,1)S(1)}, bf16[2,4,2,16,512]{4,3,2,1,0:T(8,128)(2,1)S(1)}, u32[]{:S(2)}, u32[]{:S(2)}) collective-permute-start(bf16[2,4,2,16,512]{4,3,2,1,0:T(8,128)(2,1)S(1)} %slice.19), channel_id=1, source_target_pairs={{0,3},{1,0},{2,1},{3,2},{4,7},{5,4},{6,5},{7,6},{8,11},{9,8},{10,9... | collective-permute-start | bytes 786440 | tf_op jit(solution)/shard_map/ppermute | solution.py:17
  52.0 5.8 %shard_map.83 = (f32[1,512,1024]{2,1,0:T(8,128)}, bf16[4096,1024]{1,0:T(8,128)(2,1)S(1)}, f32[512,128]{1,0:T(8,128)S(1)}, f32[8,1024]{1,0:T(8,128)S(1)}) custom-call(bf16[4,4,2,16,512]{4,3,2,1,0:T(8,128)(2,1)S(1)} %pad_maximum_fusion.refs_0_, bf16[4,4,2,16,512]{4,3,2,1,0:T(8,128)(2,1)S(1)} %pad_maximum_fusion.1.refs_1_, bf16[1,4096,1024]{2,1,0:T(8,128)(2,1)} %refs_2_.1, ...), custom_call_target="tpu_custom_call" | custom-call | tf_op jit(solution)/shard_map/pallas_call | solution.py:190
  57.8 3.9 %shard_map.84.refs_8_ = f32[1,512,1024]{2,1,0:T(8,128)} custom-call(bf16[4,4,2,16,512]{4,3,2,1,0:T(8,128)(2,1)S(1)} %collective-permute-done.4.refs_0_, bf16[4,4,2,16,512]{4,3,2,1,0:T(8,128)(2,1)S(1)} %collective-permute-done.6.refs_1_, bf16[4,4,2,16,512]{4,3,2,1,0:T(8,128)(2,1)S(1)} %collective-permute-done.12.refs_2_, ...), custom_call_target="tpu_custom_call", output_to_operand_aliasing={{}: (8, {})} | custom-call | tf_op jit(solution)/shard_map/pallas_call | solution.py:151
  61.7 2.3 %shard_map.85 = f32[1,512,1024]{2,1,0:T(8,128)} custom-call(bf16[2,4,2,16,512]{4,3,2,1,0:T(8,128)(2,1)S(1)} %collective-permute-done.5.refs_0_, bf16[2,4,2,16,512]{4,3,2,1,0:T(8,128)(2,1)S(1)} %collective-permute-done.7.refs_1_, bf16[2,4,2,16,512]{4,3,2,1,0:T(8,128)(2,1)S(1)} %collective-permute-done.13.refs_2_, ...), custom_call_target="tpu_custom_call", output_to_operand_aliasing={{}: (8, {})} | custom-call | tf_op jit(solution)/shard_map/pallas_call | solution.py:151
  (24 shorter events, 0.1 us)
Async XLA Ops:
  0.9 1.3 %collective-permute-start = (bf16[4,16,512]{2,1,0:T(8,128)(2,1)S(1)}, bf16[4,16,512]{2,1,0:T(8,128)(2,1)S(1)}, u32[]{:S(2)}, u32[]{:S(2)}) collective-permute-start(bf16[4,16,512]{2,1,0:T(8,128)(2,1)S(1)} %get-tuple-element.12), channel_id=1, source_target_pairs={{0,32},{32,0},{1,33},{33,1},{2,34},{34,2},{3,35},{35,3},{4,36},{36... | collective-permute-start | bytes 196616 | tf_op jit(solution)/shard_map/ppermute | solution.py:173
  14.2 10.6 %collective-permute-start.8 = (bf16[4,2,16,512]{3,2,1,0:T(8,128)(2,1)S(1)}, bf16[4,2,16,512]{3,2,1,0:T(8,128)(2,1)S(1)}, u32[]{:S(2)}, u32[]{:S(2)}) collective-permute-start(bf16[4,2,16,512]{3,2,1,0:T(8,128)(2,1)S(1)} %all_to_all.5), channel_id=1, source_target_pairs={{0,4},{4,0},{1,5},{5,1},{2,6},{6,2},{3,7},{7,3},{8,12},{12,8},{9,1... | collective-permute-start | bytes 393224 | tf_op jit(solution)/shard_map/ppermute | solution.py:177
  18.7 8.2 %collective-permute-start.1 = (bf16[4,2,16,512]{3,2,1,0:T(8,128)(2,1)S(1)}, bf16[4,2,16,512]{3,2,1,0:T(8,128)(2,1)S(1)}, u32[]{:S(2)}, u32[]{:S(2)}) collective-permute-start(bf16[4,2,16,512]{3,2,1,0:T(8,128)(2,1)S(1)} %all_to_all.5), channel_id=1, source_target_pairs={{0,1},{1,2},{2,3},{3,0},{4,5},{5,6},{6,7},{7,4},{8,9},{9,10},{10,1... | collective-permute-start | bytes 393224 | tf_op jit(solution)/shard_map/ppermute | solution.py:17
  20.2 9.0 %collective-permute-start.2 = (bf16[4,2,16,512]{3,2,1,0:T(8,128)(2,1)S(1)}, bf16[4,2,16,512]{3,2,1,0:T(8,128)(2,1)S(1)}, u32[]{:S(2)}, u32[]{:S(2)}) collective-permute-start(bf16[4,2,16,512]{3,2,1,0:T(8,128)(2,1)S(1)} %all_to_all.5), channel_id=1, source_target_pairs={{0,3},{1,0},{2,1},{3,2},{4,7},{5,4},{6,5},{7,6},{8,11},{9,8},{10,9... | collective-permute-start | bytes 393224 | tf_op jit(solution)/shard_map/ppermute | solution.py:17
  22.0 7.2 %collective-permute-start.3 = (bf16[4,2,16,512]{3,2,1,0:T(8,128)(2,1)S(1)}, bf16[4,2,16,512]{3,2,1,0:T(8,128)(2,1)S(1)}, u32[]{:S(2)}, u32[]{:S(2)}) collective-permute-start(bf16[4,2,16,512]{3,2,1,0:T(8,128)(2,1)S(1)} %all_to_all.5), channel_id=1, source_target_pairs={{0,2},{1,3},{2,0},{3,1},{4,6},{5,7},{6,4},{7,5},{8,10},{9,11},{10,... | collective-permute-start | bytes 393224 | tf_op jit(solution)/shard_map/ppermute | solution.py:17
  24.9 6.6 %collective-permute-start.9 = (bf16[4,2,16,512]{3,2,1,0:T(8,128)(2,1)S(1)}, bf16[4,2,16,512]{3,2,1,0:T(8,128)(2,1)S(1)}, u32[]{:S(2)}, u32[]{:S(2)}) collective-permute-start(bf16[4,2,16,512]{3,2,1,0:T(8,128)(2,1)S(1)} %collective-permute-done.8), channel_id=1, source_target_pairs={{0,8},{8,16},{16,24},{24,0},{1,9},{9,17},{17,25},{25,1},{2,10},{10... | collective-permute-start | bytes 393224 | tf_op jit(solution)/shard_map/ppermute | solution.py:17
  26.5 6.3 %collective-permute-start.10 = (bf16[4,2,16,512]{3,2,1,0:T(8,128)(2,1)S(1)}, bf16[4,2,16,512]{3,2,1,0:T(8,128)(2,1)S(1)}, u32[]{:S(2)}, u32[]{:S(2)}) collective-permute-start(bf16[4,2,16,512]{3,2,1,0:T(8,128)(2,1)S(1)} %collective-permute-done.8), channel_id=1, source_target_pairs={{0,24},{8,0},{16,8},{24,16},{1,25},{9,1},{17,9},{25,17},{2,26},{10... | collective-permute-start | bytes 393224 | tf_op jit(solution)/shard_map/ppermute | solution.py:17
  26.9 9.4 %collective-permute-start.11 = (bf16[4,2,16,512]{3,2,1,0:T(8,128)(2,1)S(1)}, bf16[4,2,16,512]{3,2,1,0:T(8,128)(2,1)S(1)}, u32[]{:S(2)}, u32[]{:S(2)}) collective-permute-start(bf16[4,2,16,512]{3,2,1,0:T(8,128)(2,1)S(1)} %collective-permute-done.8), channel_id=1, source_target_pairs={{0,16},{8,24},{16,0},{24,8},{1,17},{9,25},{17,1},{25,9},{2,18},{10... | collective-permute-start | bytes 393224 | tf_op jit(solution)/shard_map/ppermute | solution.py:17
  29.2 22.7 %copy-start.4 = (f32[200]{0:T(256)S(1)}, f32[200]{0:T(256)}, u32[]{:S(2)}) copy-start(f32[200]{0:T(256)} %param.14) | copy-start | bytes 2404
  29.2 22.7 %copy-start.3 = (f32[1800]{0:T(1024)S(1)}, f32[1800]{0:T(1024)}, u32[]{:S(2)}) copy-start(f32[1800]{0:T(1024)} %param.15) | copy-start | bytes 21604
  29.2 22.7 %copy-start = (bf16[1,512,1024]{2,1,0:T(8,128)(2,1)S(1)}, bf16[1,512,1024]{2,1,0:T(8,128)(2,1)}, u32[]{:S(2)}) copy-start(bf16[1,512,1024]{2,1,0:T(8,128)(2,1)} %refs_5_.5) | copy-start | bytes 3145732
  29.2 22.7 %copy-start.1 = (s32[1,2,1024]{2,1,0:T(2,128)S(1)}, s32[1,2,1024]{2,1,0:T(2,128)}, u32[]{:S(2)}) copy-start(s32[1,2,1024]{2,1,0:T(2,128)} %refs_5_.3) | copy-start | bytes 24580
  29.3 22.7 %copy-start.2 = (s32[1,2,512]{2,1,0:T(2,128)S(1)}, s32[1,2,512]{2,1,0:T(2,128)}, u32[]{:S(2)}) copy-start(s32[1,2,512]{2,1,0:T(2,128)} %refs_4_.1) | copy-start | bytes 12292
  29.3 13.5 %collective-permute-start.4 = (bf16[4,4,2,16,512]{4,3,2,1,0:T(8,128)(2,1)S(1)}, bf16[4,4,2,16,512]{4,3,2,1,0:T(8,128)(2,1)S(1)}, u32[]{:S(2)}, u32[]{:S(2)}) collective-permute-start(bf16[4,4,2,16,512]{4,3,2,1,0:T(8,128)(2,1)S(1)} %pad_maximum_fusion.refs_0_), channel_id=1, source_target_pairs={{0,8},{8,16},{16,24},{24,0},{1,9},{9,17},{17,25},{25,1},{2,10},{10... | collective-permute-start | bytes 1572872 | tf_op jit(solution)/shard_map/ppermute | solution.py:17
  30.3 13.7 %collective-permute-start.6 = (bf16[4,4,2,16,512]{4,3,2,1,0:T(8,128)(2,1)S(1)}, bf16[4,4,2,16,512]{4,3,2,1,0:T(8,128)(2,1)S(1)}, u32[]{:S(2)}, u32[]{:S(2)}) collective-permute-start(bf16[4,4,2,16,512]{4,3,2,1,0:T(8,128)(2,1)S(1)} %pad_maximum_fusion.refs_0_), channel_id=1, source_target_pairs={{0,24},{8,0},{16,8},{24,16},{1,25},{9,1},{17,9},{25,17},{2,26},{10... | collective-permute-start | bytes 1572872 | tf_op jit(solution)/shard_map/ppermute | solution.py:17
  36.4 12.0 %collective-permute-start.12 = (bf16[4,4,2,16,512]{4,3,2,1,0:T(8,128)(2,1)S(1)}, bf16[4,4,2,16,512]{4,3,2,1,0:T(8,128)(2,1)S(1)}, u32[]{:S(2)}, u32[]{:S(2)}) collective-permute-start(bf16[4,4,2,16,512]{4,3,2,1,0:T(8,128)(2,1)S(1)} %pad_maximum_fusion.1.refs_1_), channel_id=1, source_target_pairs={{0,1},{1,2},{2,3},{3,0},{4,5},{5,6},{6,7},{7,4},{8,9},{9,10},{10,1... | collective-permute-start | bytes 1572872 | tf_op jit(solution)/shard_map/ppermute | solution.py:17
  38.1 12.1 %collective-permute-start.14 = (bf16[4,4,2,16,512]{4,3,2,1,0:T(8,128)(2,1)S(1)}, bf16[4,4,2,16,512]{4,3,2,1,0:T(8,128)(2,1)S(1)}, u32[]{:S(2)}, u32[]{:S(2)}) collective-permute-start(bf16[4,4,2,16,512]{4,3,2,1,0:T(8,128)(2,1)S(1)} %pad_maximum_fusion.1.refs_1_), channel_id=1, source_target_pairs={{0,3},{1,0},{2,1},{3,2},{4,7},{5,4},{6,5},{7,6},{8,11},{9,8},{10,9... | collective-permute-start | bytes 1572872 | tf_op jit(solution)/shard_map/ppermute | solution.py:17
  42.9 18.8 %collective-permute-start.5 = (bf16[2,4,2,16,512]{4,3,2,1,0:T(8,128)(2,1)S(1)}, bf16[2,4,2,16,512]{4,3,2,1,0:T(8,128)(2,1)S(1)}, u32[]{:S(2)}, u32[]{:S(2)}) collective-permute-start(bf16[2,4,2,16,512]{4,3,2,1,0:T(8,128)(2,1)S(1)} %slice.16), channel_id=1, source_target_pairs={{0,8},{8,16},{16,24},{24,0},{1,9},{9,17},{17,25},{25,1},{2,10},{10... | collective-permute-start | bytes 786440 | tf_op jit(solution)/shard_map/ppermute | solution.py:17
  44.0 17.7 %collective-permute-start.7 = (bf16[2,4,2,16,512]{4,3,2,1,0:T(8,128)(2,1)S(1)}, bf16[2,4,2,16,512]{4,3,2,1,0:T(8,128)(2,1)S(1)}, u32[]{:S(2)}, u32[]{:S(2)}) collective-permute-start(bf16[2,4,2,16,512]{4,3,2,1,0:T(8,128)(2,1)S(1)} %slice.17), channel_id=1, source_target_pairs={{0,24},{8,0},{16,8},{24,16},{1,25},{9,1},{17,9},{25,17},{2,26},{10... | collective-permute-start | bytes 786440 | tf_op jit(solution)/shard_map/ppermute | solution.py:17
  48.3 13.4 %collective-permute-start.13 = (bf16[2,4,2,16,512]{4,3,2,1,0:T(8,128)(2,1)S(1)}, bf16[2,4,2,16,512]{4,3,2,1,0:T(8,128)(2,1)S(1)}, u32[]{:S(2)}, u32[]{:S(2)}) collective-permute-start(bf16[2,4,2,16,512]{4,3,2,1,0:T(8,128)(2,1)S(1)} %slice.18), channel_id=1, source_target_pairs={{0,1},{1,2},{2,3},{3,0},{4,5},{5,6},{6,7},{7,4},{8,9},{9,10},{10,1... | collective-permute-start | bytes 786440 | tf_op jit(solution)/shard_map/ppermute | solution.py:17
  50.2 11.5 %collective-permute-start.15 = (bf16[2,4,2,16,512]{4,3,2,1,0:T(8,128)(2,1)S(1)}, bf16[2,4,2,16,512]{4,3,2,1,0:T(8,128)(2,1)S(1)}, u32[]{:S(2)}, u32[]{:S(2)}) collective-permute-start(bf16[2,4,2,16,512]{4,3,2,1,0:T(8,128)(2,1)S(1)} %slice.19), channel_id=1, source_target_pairs={{0,3},{1,0},{2,1},{3,2},{4,7},{5,4},{6,5},{7,6},{8,11},{9,8},{10,9... | collective-permute-start | bytes 786440 | tf_op jit(solution)/shard_map/ppermute | solution.py:17

commit v3 on v2

--- a/solution.py
+++ b/solution.py
@@ -10,6 +10,7 @@
 ROW, COL = ("zlo", "core"), ("y", "zhi", "x")
 TILE = 256
 TILES = 1024 // TILE
+STEP = 64
 NEAR = (0, 3, 1, 2)
 
 
@@ -22,17 +23,6 @@
     ahead = send(block, axis, -1)
     far = send(block, axis, 2)
     return jnp.stack([block, back, ahead, far])
-
-
-def live_kernel(counts_ref, amplitudes_ref, keep_ref, pass_ref):
-    core = lax.axis_index("core")
-    width = amplitudes_ref.shape[2]
-    first = (lax.axis_index("zlo") * 2 + core) * width
-    position = first + lax.broadcasted_iota(jnp.int32, (16, width), 1)
-    for z in range(4):
-        for out_ref, irrep in ((keep_ref, z * 2 + core), (pass_ref, z * 2 + 1 - core)):
-            block = amplitudes_ref[irrep]
-            out_ref[z] = jnp.where(position < counts_ref[irrep], block, jnp.zeros_like(block))
 
 
 def pick(table_ref, index):
@@ -64,12 +54,9 @@
 
 
 def update(groups, refs, held_ref, bare_ref, occ_sum_ref, vir_sum_ref, out_ref, live_ref, stage_ref, sem, ready=None):
-    core = lax.axis_index("core")
     for g, (number, k, _, _, _) in enumerate(groups):
-        for z in range(4):
-            for c in range(2):
-                panel = pl.multiple_of((z * 2 + (core + c) % 2) * 512, 512)
-                live_ref[g * 16 : (g + 1) * 16, pl.ds(panel, 512)] = refs[number][k, z, c]
+        for p in range(8):
+            live_ref[g * 16 : (g + 1) * 16, p * 512 : (p + 1) * 512] = refs[number][k, p]
     copies = []
     for n in range(TILES):
         tile = slice(n * TILE, (n + 1) * TILE)
@@ -96,8 +83,8 @@
 
 
 def own_kernel(*refs):
-    (integrals_ref, bare_ref, ij_ref, ab_ref, occ_ref, vir_ref) = refs[2:8]
-    (out_ref, held_ref, occ_sum_ref, vir_sum_ref, live_ref, stage_ref, sem, load_sem) = refs[8:]
+    (counts_ref, integrals_ref, bare_ref, ij_ref, ab_ref, occ_ref, vir_ref) = refs[2:9]
+    (out_ref, held_ref, occ_sum_ref, vir_sum_ref, live_ref, stage_ref, sem, load_sem) = refs[9:]
     loads = []
     for n in range(TILES):
         tile = pl.ds(n * TILE, TILE)
@@ -115,9 +102,27 @@
         for side in range(2):
             vir = vir + pick(vir_ref, jnp.broadcast_to(ab_ref[0, side : side + 1, cols], (8, 128)))
         vir_sum_ref[:, cols] = vir
+    count = counts_ref[lax.axis_index(ROW)]
+
+    def ready(n):
+        loads[n].wait()
+        tile = slice(n * TILE, (n + 1) * TILE)
+        edge = count // STEP
+        blank = jnp.zeros((STEP, TILE), held_ref.dtype)
+
+        @pl.when(count < 4096)
+        def _():
+            rows = pl.ds(pl.multiple_of(edge * STEP, STEP), STEP)
+            slots = edge * STEP + lax.broadcasted_iota(jnp.int32, (STEP, TILE), 0)
+            held_ref[rows, tile] = jnp.where(slots < count, held_ref[rows, tile], blank)
+
+        @pl.loop(edge + 1, 4096 // STEP)
+        def _(step):
+            held_ref[pl.ds(pl.multiple_of(step * STEP, STEP), STEP), tile] = blank
+
     update(
         OWN, refs[:2], held_ref, bare_ref, occ_sum_ref, vir_sum_ref, out_ref, live_ref, stage_ref, sem,
-        ready=lambda n: loads[n].wait(),
+        ready=ready,
     )
 
 
@@ -127,9 +132,16 @@
     update(groups, refs[:count], held_ref, bare_ref, occ_sum_ref, vir_sum_ref, out_ref, live_ref, stage_ref, sem)
 
 
+def split_kernel(back_ref, ahead_ref, after_ref, low_ref, high_ref):
+    low_ref[...] = back_ref[:2]
+    high_ref[...] = ahead_ref[2:]
+
+
 IN_VMEM = pl.BlockSpec(memory_space=pltpu.VMEM)
+IN_SMEM = pl.BlockSpec(memory_space=pltpu.SMEM)
 IN_HBM = pl.BlockSpec(memory_space=pl.ANY)
 PARAMS = pltpu.CompilerParams(vmem_limit_bytes=16 * 1024 * 1024)
+SMALL = pltpu.CompilerParams(vmem_limit_bytes=2 * 1024 * 1024)
 RESULT = jax.ShapeDtypeStruct((1, 512, 1024), jnp.float32)
 
 
@@ -159,37 +171,36 @@
     )(*[in_vmem(p) for p in pieces], held, bare, occ_sum, vir_sum, begun)
 
 
+def relayed(back, ahead, after):
+    half = pltpu.VMEM((2, *back.shape[1:]), back.dtype)
+    return pl.pallas_call(
+        split_kernel,
+        in_specs=[IN_VMEM] * 2 + [IN_HBM],
+        out_specs=(IN_VMEM, IN_VMEM),
+        out_shape=(half, half),
+        compiler_params=SMALL,
+    )(in_vmem(back), in_vmem(ahead), after)
+
+
 def on_device(
     amplitudes, integrals, bare, cd_count, ij_orbitals, ab_orbitals, occ_energy, vir_energy
 ):
-    width = amplitudes.shape[2]
-    piece = pltpu.VMEM((4, 16, width), amplitudes.dtype)
-    kept, passed = pl.pallas_call(
-        live_kernel,
-        out_shape=(piece, piece),
-        in_specs=[pl.BlockSpec(memory_space=pltpu.SMEM), IN_VMEM],
-        out_specs=(IN_VMEM, IN_VMEM),
-    )(cd_count, amplitudes)
-    given = lax.ppermute(passed, "core", [(0, 1), (1, 0)])
-    own = lax.all_to_all(
-        jnp.stack([kept, given], axis=1), "zlo", split_axis=0, concat_axis=0, tiled=True
-    )
+    own = lax.all_to_all(amplitudes, ROW, split_axis=0, concat_axis=0, tiled=True)
     other = lax.ppermute(own, "zhi", [(0, 1), (1, 0)])
-    stacks, beside, far = [], [], []
+    stacks, beside = [], []
     for block, one, two in ((own, "x", "y"), (other, "y", "x")):
         blocks = near(block, one)
         back = send(blocks, two, 1)
         ahead = send(blocks, two, -1)
         stacks.append(blocks)
         beside += [back, ahead]
-        far += [send(back[:2], two, 1), send(ahead[2:], two, -1)]
 
     occ_table = jnp.pad(occ_energy, (0, 56)).reshape(2, 128)
     vir_table = jnp.pad(vir_energy, (0, 120)).reshape(15, 128)
     bare = in_vmem(bare)
     begun, held, occ_sum, vir_sum = pl.pallas_call(
         own_kernel,
-        in_specs=[IN_VMEM] * 2 + [IN_HBM] + [IN_VMEM] * 5,
+        in_specs=[IN_VMEM] * 2 + [IN_SMEM, IN_HBM] + [IN_VMEM] * 5,
         out_specs=[IN_HBM, IN_VMEM, IN_VMEM, IN_VMEM],
         out_shape=(
             RESULT,
@@ -201,9 +212,14 @@
         compiler_params=PARAMS,
     )(
         *[in_vmem(p) for p in stacks],
+        cd_count,
         pltpu.with_memory_space_constraint(integrals, pltpu.HBM),
         bare, ij_orbitals, ab_orbitals, occ_table, vir_table,
     )
+    far = []
+    for half, axis in enumerate(("y", "x")):
+        low, high = relayed(beside[half * 2], beside[half * 2 + 1], vir_sum)
+        far += [send(low, axis, 1), send(high, axis, -1)]
     begun = more(BESIDE, beside, held, bare, occ_sum, vir_sum, begun)
     return more(FAR, far, held, bare, occ_sum, vir_sum, begun)
 

time: 64.3 us -> 61.2 us (0.952); the launches traced: 64.2 us -> 60.3 us
  waiting for transfers between devices: 13.6 us -> 8.62 us
  Pallas kernels: 13 us -> 13.9 us
  blocking collectives: 11.9 us -> 12.8 us
    ppermute x14, waiting for transfers between devices: 11.3 us -> 6.6 us  [send(): return lax.ppermute(block, axis, [(i, (i + shift) % 4) for i in range(4)])]
    ppermute x1 -> x0, waiting for transfers between devices: 1.24 us -> none  [on_device(): given = lax.ppermute(passed, 'core', [(0, 1), (1, 0)])]
    pallas_call x2 -> x3, Pallas kernels: 6.74 us -> 7.82 us  [the longest x1 7.75 us: on_device(): pl.pallas_call(own_kernel, in_specs=[IN_VMEM] * 2 + [IN_SMEM, IN_HBM] + [...]
    ppermute x1, waiting for transfers between devices: 1.1 us -> 2.02 us  [on_device(): other = lax.ppermute(own, 'zhi', [(0, 1), (1, 0)])]
    all_to_all x1, blocking collectives: 11.9 us -> 12.8 us  [on_device(): lax.all_to_all(amplitudes, ROW, split_axis=0, concat_axis=0, tiled=True)]
  transfers between devices with their start and end apart: 16 -> 15, of which waited for: 6 -> 6; matrix products, arithmetic and copies ran while one was open for 0% -> 0% of each run, Pallas kernels for 15% -> 19%
where the time goes in v3:
time: 61.2 us; the launch traced here: 60.3 us
  starting transfers between devices  24.5 us (40%)
  Pallas kernels  13.9 us (23%)
  blocking collectives  12.8 us (21%)
  waiting for transfers between devices  8.62 us (14%)
    ppermute x14, starting transfers between devices, send(): return lax.ppermute(block, axis, [(i, (i + shift) % 4) for i in range(4)])  19.9 us
    all_to_all x1, blocking collectives, on_device(): lax.all_to_all(amplitudes, ROW, split_axis=0, concat_axis=0, tiled=True)  12.8 us
    pallas_call x1, Pallas kernels, on_device(): pl.pallas_call(own_kernel, in_specs=[IN_VMEM] * 2 + [IN_SMEM, IN_HBM] + [...  7.75 us
    ppermute x14, waiting for transfers between devices, send(): return lax.ppermute(block, axis, [(i, (i + shift) % 4) for i in range(4)])  6.6 us
    pallas_call x2, Pallas kernels, more(): pl.pallas_call(functools.partial(more_kernel, groups), in_specs=[IN_VMEM]...  6.1 us
    ppermute x1, starting transfers between devices, on_device(): other = lax.ppermute(own, 'zhi', [(0, 1), (1, 0)])  4.57 us
    ppermute x1, waiting for transfers between devices, on_device(): other = lax.ppermute(own, 'zhi', [(0, 1), (1, 0)])  2.02 us
  transfers between devices with their start and end apart: 15, of which 6 were waited for; matrix products, arithmetic and copies ran while one was open for 0% of the time, Pallas kernels for 19%

profile of v3, /device:TPU:8, one launch (start us, length us, event | category | flops | bytes accessed | tf_op | source)
XLA Modules:
  0.0 60.3 jit_solution(13076558127038644830)
XLA Ops:
  0.0 12.8 %all_to_all.5 = bf16[8,16,512]{2,1,0:T(8,128)(2,1)S(1)} all-to-all(bf16[8,16,512]{2,1,0:T(8,128)(2,1)} %param.8), channel_id=1, replica_groups=mesh['zlo'=4,'core'=2,'y'=4,'zhi'=2,'x'=4] {'zlo','core'}, dimensions={0} | all-to-all | bytes 262144 | tf_op jit(solution)/shard_map/all_to_all | solution.py:188
  12.9 4.6 %collective-permute-start.5 = (bf16[8,16,512]{2,1,0:T(8,128)(2,1)S(1)}, bf16[8,16,512]{2,1,0:T(8,128)(2,1)S(1)}, u32[]{:S(2)}, u32[]{:S(2)}) collective-permute-start(bf16[8,16,512]{2,1,0:T(8,128)(2,1)S(1)} %all_to_all.5), channel_id=1, source_target_pairs={{0,4},{4,0},{1,5},{5,1},{2,6},{6,2},{3,7},{7,3},{8,12},{12,8},{9,1... | collective-permute-start | bytes 393224 | tf_op jit(solution)/shard_map/ppermute | solution.py:189
  17.4 3.0 %collective-permute-start.2 = (bf16[8,16,512]{2,1,0:T(8,128)(2,1)S(1)}, bf16[8,16,512]{2,1,0:T(8,128)(2,1)S(1)}, u32[]{:S(2)}, u32[]{:S(2)}) collective-permute-start(bf16[8,16,512]{2,1,0:T(8,128)(2,1)S(1)} %all_to_all.5), channel_id=1, source_target_pairs={{0,2},{1,3},{2,0},{3,1},{4,6},{5,7},{6,4},{7,5},{8,10},{9,11},{10,... | collective-permute-start | bytes 393224 | tf_op jit(solution)/shard_map/ppermute | solution.py:18
  20.5 1.1 %collective-permute-start.1 = (bf16[8,16,512]{2,1,0:T(8,128)(2,1)S(1)}, bf16[8,16,512]{2,1,0:T(8,128)(2,1)S(1)}, u32[]{:S(2)}, u32[]{:S(2)}) collective-permute-start(bf16[8,16,512]{2,1,0:T(8,128)(2,1)S(1)} %all_to_all.5), channel_id=1, source_target_pairs={{0,3},{1,0},{2,1},{3,2},{4,7},{5,4},{6,5},{7,6},{8,11},{9,8},{10,9... | collective-permute-start | bytes 393224 | tf_op jit(solution)/shard_map/ppermute | solution.py:18
  21.6 0.9 %collective-permute-start = (bf16[8,16,512]{2,1,0:T(8,128)(2,1)S(1)}, bf16[8,16,512]{2,1,0:T(8,128)(2,1)S(1)}, u32[]{:S(2)}, u32[]{:S(2)}) collective-permute-start(bf16[8,16,512]{2,1,0:T(8,128)(2,1)S(1)} %all_to_all.5), channel_id=1, source_target_pairs={{0,1},{1,2},{2,3},{3,0},{4,5},{5,6},{6,7},{7,4},{8,9},{9,10},{10,1... | collective-permute-start | bytes 393224 | tf_op jit(solution)/shard_map/ppermute | solution.py:18
  22.5 2.0 %collective-permute-done.5 = bf16[8,16,512]{2,1,0:T(8,128)(2,1)S(1)} collective-permute-done((bf16[8,16,512]{2,1,0:T(8,128)(2,1)S(1)}, bf16[8,16,512]{2,1,0:T(8,128)(2,1)S(1)}, u32[]{:S(2)}, u32[]{:S(2)}) %collective-permute-start.5) | collective-permute-done | bytes 131104 | tf_op jit(solution)/shard_map/ppermute | solution.py:189
  24.5 2.3 %collective-permute-start.8 = (bf16[8,16,512]{2,1,0:T(8,128)(2,1)S(1)}, bf16[8,16,512]{2,1,0:T(8,128)(2,1)S(1)}, u32[]{:S(2)}, u32[]{:S(2)}) collective-permute-start(bf16[8,16,512]{2,1,0:T(8,128)(2,1)S(1)} %collective-permute-done.5), channel_id=1, source_target_pairs={{0,16},{8,24},{16,0},{24,8},{1,17},{9,25},{17,1},{25,9},{2,18},{10... | collective-permute-start | bytes 393224 | tf_op jit(solution)/shard_map/ppermute | solution.py:18
  26.8 1.3 %collective-permute-start.7 = (bf16[8,16,512]{2,1,0:T(8,128)(2,1)S(1)}, bf16[8,16,512]{2,1,0:T(8,128)(2,1)S(1)}, u32[]{:S(2)}, u32[]{:S(2)}) collective-permute-start(bf16[8,16,512]{2,1,0:T(8,128)(2,1)S(1)} %collective-permute-done.5), channel_id=1, source_target_pairs={{0,24},{8,0},{16,8},{24,16},{1,25},{9,1},{17,9},{25,17},{2,26},{10... | collective-permute-start | bytes 393224 | tf_op jit(solution)/shard_map/ppermute | solution.py:18
  28.1 0.0 collective-permute-done.2
  28.1 0.7 %collective-permute-start.6 = (bf16[8,16,512]{2,1,0:T(8,128)(2,1)S(1)}, bf16[8,16,512]{2,1,0:T(8,128)(2,1)S(1)}, u32[]{:S(2)}, u32[]{:S(2)}) collective-permute-start(bf16[8,16,512]{2,1,0:T(8,128)(2,1)S(1)} %collective-permute-done.5), channel_id=1, source_target_pairs={{0,8},{8,16},{16,24},{24,0},{1,9},{9,17},{17,25},{25,1},{2,10},{10... | collective-permute-start | bytes 393224 | tf_op jit(solution)/shard_map/ppermute | solution.py:18
  28.8 0.0 collective-permute-done.1
  28.8 0.0 collective-permute-done
  28.8 0.1 pad_maximum_fusion.refs_0_
  28.9 1.4 %collective-permute-start.4 = (bf16[4,8,16,512]{3,2,1,0:T(8,128)(2,1)S(1)}, bf16[4,8,16,512]{3,2,1,0:T(8,128)(2,1)S(1)}, u32[]{:S(2)}, u32[]{:S(2)}) collective-permute-start(bf16[4,8,16,512]{3,2,1,0:T(8,128)(2,1)S(1)} %pad_maximum_fusion.refs_0_), channel_id=1, source_target_pairs={{0,24},{8,0},{16,8},{24,16},{1,25},{9,1},{17,9},{25,17},{2,26},{10... | collective-permute-start | bytes 1572872 | tf_op jit(solution)/shard_map/ppermute | solution.py:18
  30.3 0.7 %collective-permute-start.3 = (bf16[4,8,16,512]{3,2,1,0:T(8,128)(2,1)S(1)}, bf16[4,8,16,512]{3,2,1,0:T(8,128)(2,1)S(1)}, u32[]{:S(2)}, u32[]{:S(2)}) collective-permute-start(bf16[4,8,16,512]{3,2,1,0:T(8,128)(2,1)S(1)} %pad_maximum_fusion.refs_0_), channel_id=1, source_target_pairs={{0,8},{8,16},{16,24},{24,0},{1,9},{9,17},{17,25},{25,1},{2,10},{10... | collective-permute-start | bytes 1572872 | tf_op jit(solution)/shard_map/ppermute | solution.py:18
  31.0 1.3 %collective-permute-done.8 = bf16[8,16,512]{2,1,0:T(8,128)(2,1)S(1)} collective-permute-done((bf16[8,16,512]{2,1,0:T(8,128)(2,1)S(1)}, bf16[8,16,512]{2,1,0:T(8,128)(2,1)S(1)}, u32[]{:S(2)}, u32[]{:S(2)}) %collective-permute-start.8) | collective-permute-done | bytes 131104 | tf_op jit(solution)/shard_map/ppermute | solution.py:18
  32.3 1.9 %collective-permute-done.7 = bf16[8,16,512]{2,1,0:T(8,128)(2,1)S(1)} collective-permute-done((bf16[8,16,512]{2,1,0:T(8,128)(2,1)S(1)}, bf16[8,16,512]{2,1,0:T(8,128)(2,1)S(1)}, u32[]{:S(2)}, u32[]{:S(2)}) %collective-permute-start.7) | collective-permute-done | bytes 131104 | tf_op jit(solution)/shard_map/ppermute | solution.py:18
  34.2 0.8 %collective-permute-done.6 = bf16[8,16,512]{2,1,0:T(8,128)(2,1)S(1)} collective-permute-done((bf16[8,16,512]{2,1,0:T(8,128)(2,1)S(1)}, bf16[8,16,512]{2,1,0:T(8,128)(2,1)S(1)}, u32[]{:S(2)}, u32[]{:S(2)}) %collective-permute-start.6) | collective-permute-done | bytes 131104 | tf_op jit(solution)/shard_map/ppermute | solution.py:18
  35.0 0.1 pad_maximum_fusion.1.refs_1_
  35.1 3.0 %collective-permute-start.12 = (bf16[4,8,16,512]{3,2,1,0:T(8,128)(2,1)S(1)}, bf16[4,8,16,512]{3,2,1,0:T(8,128)(2,1)S(1)}, u32[]{:S(2)}, u32[]{:S(2)}) collective-permute-start(bf16[4,8,16,512]{3,2,1,0:T(8,128)(2,1)S(1)} %pad_maximum_fusion.1.refs_1_), channel_id=1, source_target_pairs={{0,3},{1,0},{2,1},{3,2},{4,7},{5,4},{6,5},{7,6},{8,11},{9,8},{10,9... | collective-permute-start | bytes 1572872 | tf_op jit(solution)/shard_map/ppermute | solution.py:18
  38.2 7.7 %shard_map.82 = (f32[1,512,1024]{2,1,0:T(8,128)}, bf16[4096,1024]{1,0:T(8,128)(2,1)S(1)}, f32[512,128]{1,0:T(8,128)S(1)}, f32[8,1024]{1,0:T(8,128)S(1)}) custom-call(bf16[4,8,16,512]{3,2,1,0:T(8,128)(2,1)S(1)} %pad_maximum_fusion.refs_0_, bf16[4,8,16,512]{3,2,1,0:T(8,128)(2,1)S(1)} %pad_maximum_fusion.1.refs_1_, s32[8]{0:T(128)S(1)} %copy-done.3, ...), custom_call_target="tpu_custom_call" | custom-call | tf_op jit(solution)/shard_map/pallas_call | solution.py:201
  46.0 0.0 collective-permute-done.3.back_ref.refs_0_
  46.0 0.9 %collective-permute-start.9 = (bf16[2,8,16,512]{3,2,1,0:T(8,128)(2,1)S(1)}, bf16[2,8,16,512]{3,2,1,0:T(8,128)(2,1)S(1)}, u32[]{:S(2)}, u32[]{:S(2)}) collective-permute-start(bf16[2,8,16,512]{3,2,1,0:T(8,128)(2,1)S(1)} %get-tuple-element.14), channel_id=1, source_target_pairs={{0,8},{8,16},{16,24},{24,0},{1,9},{9,17},{17,25},{25,1},{2,10},{10... | collective-permute-start | bytes 786440 | tf_op jit(solution)/shard_map/ppermute | solution.py:18
  46.9 1.3 %collective-permute-start.10 = (bf16[2,8,16,512]{3,2,1,0:T(8,128)(2,1)S(1)}, bf16[2,8,16,512]{3,2,1,0:T(8,128)(2,1)S(1)}, u32[]{:S(2)}, u32[]{:S(2)}) collective-permute-start(bf16[2,8,16,512]{3,2,1,0:T(8,128)(2,1)S(1)} %get-tuple-element.15), channel_id=1, source_target_pairs={{0,24},{8,0},{16,8},{24,16},{1,25},{9,1},{17,9},{25,17},{2,26},{10... | collective-permute-start | bytes 786440 | tf_op jit(solution)/shard_map/ppermute | solution.py:18
  48.1 0.0 collective-permute-done.12.ahead_ref.refs_3_
  48.1 2.1 %collective-permute-done.11.back_ref.refs_2_ = bf16[4,8,16,512]{3,2,1,0:T(8,128)(2,1)S(1)} collective-permute-done((bf16[4,8,16,512]{3,2,1,0:T(8,128)(2,1)S(1)}, bf16[4,8,16,512]{3,2,1,0:T(8,128)(2,1)S(1)}, u32[]{:S(2)}, u32[]{:S(2)}) %collective-permute-start.11) | collective-permute-done | bytes 524320 | tf_op jit(solution)/shard_map/ppermute | solution.py:18
  50.2 0.1 collective-permute-start.13
  50.3 3.2 %collective-permute-start.14 = (bf16[2,8,16,512]{3,2,1,0:T(8,128)(2,1)S(1)}, bf16[2,8,16,512]{3,2,1,0:T(8,128)(2,1)S(1)}, u32[]{:S(2)}, u32[]{:S(2)}) collective-permute-start(bf16[2,8,16,512]{3,2,1,0:T(8,128)(2,1)S(1)} %get-tuple-element.17), channel_id=1, source_target_pairs={{0,3},{1,0},{2,1},{3,2},{4,7},{5,4},{6,5},{7,6},{8,11},{9,8},{10,9... | collective-permute-start | bytes 786440 | tf_op jit(solution)/shard_map/ppermute | solution.py:18
  53.6 3.8 %shard_map.85.refs_8_ = f32[1,512,1024]{2,1,0:T(8,128)} custom-call(bf16[4,8,16,512]{3,2,1,0:T(8,128)(2,1)S(1)} %collective-permute-done.3.back_ref.refs_0_, bf16[4,8,16,512]{3,2,1,0:T(8,128)(2,1)S(1)} %collective-permute-done.4.ahead_ref.refs_1_, ...), custom_call_target="tpu_custom_call", output_to_operand_aliasing={{}: (8, {})} | custom-call | tf_op jit(solution)/shard_map/pallas_call | solution.py:163
  57.4 0.0 collective-permute-done.9.refs_0_
  57.4 0.5 collective-permute-done.13.refs_2_
  57.9 2.3 %shard_map.86 = f32[1,512,1024]{2,1,0:T(8,128)} custom-call(bf16[2,8,16,512]{3,2,1,0:T(8,128)(2,1)S(1)} %collective-permute-done.9.refs_0_, bf16[2,8,16,512]{3,2,1,0:T(8,128)(2,1)S(1)} %collective-permute-done.10.refs_1_, bf16[2,8,16,512]{3,2,1,0:T(8,128)(2,1)S(1)} %collective-permute-done.13.refs_2_, ...), custom_call_target="tpu_custom_call", output_to_operand_aliasing={{}: (8, {})} | custom-call | tf_op jit(solution)/shard_map/pallas_call | solution.py:163
  (20 shorter events, 0.1 us)
Async XLA Ops:
  0.0 38.1 %copy-start.5 = (f32[200]{0:T(256)S(1)}, f32[200]{0:T(256)}, u32[]{:S(2)}) copy-start(f32[200]{0:T(256)} %param.14) | copy-start | bytes 2404
  0.0 38.2 %copy-start.4 = (f32[1800]{0:T(1024)S(1)}, f32[1800]{0:T(1024)}, u32[]{:S(2)}) copy-start(f32[1800]{0:T(1024)} %param.15) | copy-start | bytes 21604
  0.0 38.2 %copy-start = (bf16[1,512,1024]{2,1,0:T(8,128)(2,1)S(1)}, bf16[1,512,1024]{2,1,0:T(8,128)(2,1)}, u32[]{:S(2)}) copy-start(bf16[1,512,1024]{2,1,0:T(8,128)(2,1)} %refs_5_.5) | copy-start | bytes 3145732
  0.0 38.2 %copy-start.1 = (s32[1,2,1024]{2,1,0:T(2,128)S(1)}, s32[1,2,1024]{2,1,0:T(2,128)}, u32[]{:S(2)}) copy-start(s32[1,2,1024]{2,1,0:T(2,128)} %refs_6_.1) | copy-start | bytes 24580
  0.0 38.2 %copy-start.2 = (s32[1,2,512]{2,1,0:T(2,128)S(1)}, s32[1,2,512]{2,1,0:T(2,128)}, u32[]{:S(2)}) copy-start(s32[1,2,512]{2,1,0:T(2,128)} %refs_5_.3) | copy-start | bytes 12292
  0.0 38.2 %copy-start.3 = (s32[8]{0:T(128)S(1)}, s32[8]{0:T(128)}, u32[]{:S(2)}) copy-start(s32[8]{0:T(128)} %refs_2_.1) | copy-start | bytes 100
  12.9 11.6 %collective-permute-start.5 = (bf16[8,16,512]{2,1,0:T(8,128)(2,1)S(1)}, bf16[8,16,512]{2,1,0:T(8,128)(2,1)S(1)}, u32[]{:S(2)}, u32[]{:S(2)}) collective-permute-start(bf16[8,16,512]{2,1,0:T(8,128)(2,1)S(1)} %all_to_all.5), channel_id=1, source_target_pairs={{0,4},{4,0},{1,5},{5,1},{2,6},{6,2},{3,7},{7,3},{8,12},{12,8},{9,1... | collective-permute-start | bytes 393224 | tf_op jit(solution)/shard_map/ppermute | solution.py:189
  17.4 10.7 %collective-permute-start.2 = (bf16[8,16,512]{2,1,0:T(8,128)(2,1)S(1)}, bf16[8,16,512]{2,1,0:T(8,128)(2,1)S(1)}, u32[]{:S(2)}, u32[]{:S(2)}) collective-permute-start(bf16[8,16,512]{2,1,0:T(8,128)(2,1)S(1)} %all_to_all.5), channel_id=1, source_target_pairs={{0,2},{1,3},{2,0},{3,1},{4,6},{5,7},{6,4},{7,5},{8,10},{9,11},{10,... | collective-permute-start | bytes 393224 | tf_op jit(solution)/shard_map/ppermute | solution.py:18
  20.5 8.4 %collective-permute-start.1 = (bf16[8,16,512]{2,1,0:T(8,128)(2,1)S(1)}, bf16[8,16,512]{2,1,0:T(8,128)(2,1)S(1)}, u32[]{:S(2)}, u32[]{:S(2)}) collective-permute-start(bf16[8,16,512]{2,1,0:T(8,128)(2,1)S(1)} %all_to_all.5), channel_id=1, source_target_pairs={{0,3},{1,0},{2,1},{3,2},{4,7},{5,4},{6,5},{7,6},{8,11},{9,8},{10,9... | collective-permute-start | bytes 393224 | tf_op jit(solution)/shard_map/ppermute | solution.py:18
  21.6 7.2 %collective-permute-start = (bf16[8,16,512]{2,1,0:T(8,128)(2,1)S(1)}, bf16[8,16,512]{2,1,0:T(8,128)(2,1)S(1)}, u32[]{:S(2)}, u32[]{:S(2)}) collective-permute-start(bf16[8,16,512]{2,1,0:T(8,128)(2,1)S(1)} %all_to_all.5), channel_id=1, source_target_pairs={{0,1},{1,2},{2,3},{3,0},{4,5},{5,6},{6,7},{7,4},{8,9},{9,10},{10,1... | collective-permute-start | bytes 393224 | tf_op jit(solution)/shard_map/ppermute | solution.py:18
  24.5 7.8 %collective-permute-start.8 = (bf16[8,16,512]{2,1,0:T(8,128)(2,1)S(1)}, bf16[8,16,512]{2,1,0:T(8,128)(2,1)S(1)}, u32[]{:S(2)}, u32[]{:S(2)}) collective-permute-start(bf16[8,16,512]{2,1,0:T(8,128)(2,1)S(1)} %collective-permute-done.5), channel_id=1, source_target_pairs={{0,16},{8,24},{16,0},{24,8},{1,17},{9,25},{17,1},{25,9},{2,18},{10... | collective-permute-start | bytes 393224 | tf_op jit(solution)/shard_map/ppermute | solution.py:18
  26.8 7.4 %collective-permute-start.7 = (bf16[8,16,512]{2,1,0:T(8,128)(2,1)S(1)}, bf16[8,16,512]{2,1,0:T(8,128)(2,1)S(1)}, u32[]{:S(2)}, u32[]{:S(2)}) collective-permute-start(bf16[8,16,512]{2,1,0:T(8,128)(2,1)S(1)} %collective-permute-done.5), channel_id=1, source_target_pairs={{0,24},{8,0},{16,8},{24,16},{1,25},{9,1},{17,9},{25,17},{2,26},{10... | collective-permute-start | bytes 393224 | tf_op jit(solution)/shard_map/ppermute | solution.py:18
  28.1 6.9 %collective-permute-start.6 = (bf16[8,16,512]{2,1,0:T(8,128)(2,1)S(1)}, bf16[8,16,512]{2,1,0:T(8,128)(2,1)S(1)}, u32[]{:S(2)}, u32[]{:S(2)}) collective-permute-start(bf16[8,16,512]{2,1,0:T(8,128)(2,1)S(1)} %collective-permute-done.5), channel_id=1, source_target_pairs={{0,8},{8,16},{16,24},{24,0},{1,9},{9,17},{17,25},{25,1},{2,10},{10... | collective-permute-start | bytes 393224 | tf_op jit(solution)/shard_map/ppermute | solution.py:18
  28.9 17.1 %collective-permute-start.4 = (bf16[4,8,16,512]{3,2,1,0:T(8,128)(2,1)S(1)}, bf16[4,8,16,512]{3,2,1,0:T(8,128)(2,1)S(1)}, u32[]{:S(2)}, u32[]{:S(2)}) collective-permute-start(bf16[4,8,16,512]{3,2,1,0:T(8,128)(2,1)S(1)} %pad_maximum_fusion.refs_0_), channel_id=1, source_target_pairs={{0,24},{8,0},{16,8},{24,16},{1,25},{9,1},{17,9},{25,17},{2,26},{10... | collective-permute-start | bytes 1572872 | tf_op jit(solution)/shard_map/ppermute | solution.py:18
  30.3 15.7 %collective-permute-start.3 = (bf16[4,8,16,512]{3,2,1,0:T(8,128)(2,1)S(1)}, bf16[4,8,16,512]{3,2,1,0:T(8,128)(2,1)S(1)}, u32[]{:S(2)}, u32[]{:S(2)}) collective-permute-start(bf16[4,8,16,512]{3,2,1,0:T(8,128)(2,1)S(1)} %pad_maximum_fusion.refs_0_), channel_id=1, source_target_pairs={{0,8},{8,16},{16,24},{24,0},{1,9},{9,17},{17,25},{25,1},{2,10},{10... | collective-permute-start | bytes 1572872 | tf_op jit(solution)/shard_map/ppermute | solution.py:18
  35.1 13.0 %collective-permute-start.12 = (bf16[4,8,16,512]{3,2,1,0:T(8,128)(2,1)S(1)}, bf16[4,8,16,512]{3,2,1,0:T(8,128)(2,1)S(1)}, u32[]{:S(2)}, u32[]{:S(2)}) collective-permute-start(bf16[4,8,16,512]{3,2,1,0:T(8,128)(2,1)S(1)} %pad_maximum_fusion.1.refs_1_), channel_id=1, source_target_pairs={{0,3},{1,0},{2,1},{3,2},{4,7},{5,4},{6,5},{7,6},{8,11},{9,8},{10,9... | collective-permute-start | bytes 1572872 | tf_op jit(solution)/shard_map/ppermute | solution.py:18
  38.1 12.1 %collective-permute-start.11 = (bf16[4,8,16,512]{3,2,1,0:T(8,128)(2,1)S(1)}, bf16[4,8,16,512]{3,2,1,0:T(8,128)(2,1)S(1)}, u32[]{:S(2)}, u32[]{:S(2)}) collective-permute-start(bf16[4,8,16,512]{3,2,1,0:T(8,128)(2,1)S(1)} %pad_maximum_fusion.1.refs_1_), channel_id=1, source_target_pairs={{0,1},{1,2},{2,3},{3,0},{4,5},{5,6},{6,7},{7,4},{8,9},{9,10},{10,1... | collective-permute-start | bytes 1572872 | tf_op jit(solution)/shard_map/ppermute | solution.py:18
  46.0 11.4 %collective-permute-start.9 = (bf16[2,8,16,512]{3,2,1,0:T(8,128)(2,1)S(1)}, bf16[2,8,16,512]{3,2,1,0:T(8,128)(2,1)S(1)}, u32[]{:S(2)}, u32[]{:S(2)}) collective-permute-start(bf16[2,8,16,512]{3,2,1,0:T(8,128)(2,1)S(1)} %get-tuple-element.14), channel_id=1, source_target_pairs={{0,8},{8,16},{16,24},{24,0},{1,9},{9,17},{17,25},{25,1},{2,10},{10... | collective-permute-start | bytes 786440 | tf_op jit(solution)/shard_map/ppermute | solution.py:18
  46.9 10.5 %collective-permute-start.10 = (bf16[2,8,16,512]{3,2,1,0:T(8,128)(2,1)S(1)}, bf16[2,8,16,512]{3,2,1,0:T(8,128)(2,1)S(1)}, u32[]{:S(2)}, u32[]{:S(2)}) collective-permute-start(bf16[2,8,16,512]{3,2,1,0:T(8,128)(2,1)S(1)} %get-tuple-element.15), channel_id=1, source_target_pairs={{0,24},{8,0},{16,8},{24,16},{1,25},{9,1},{17,9},{25,17},{2,26},{10... | collective-permute-start | bytes 786440 | tf_op jit(solution)/shard_map/ppermute | solution.py:18
  50.2 7.7 %collective-permute-start.13 = (bf16[2,8,16,512]{3,2,1,0:T(8,128)(2,1)S(1)}, bf16[2,8,16,512]{3,2,1,0:T(8,128)(2,1)S(1)}, u32[]{:S(2)}, u32[]{:S(2)}) collective-permute-start(bf16[2,8,16,512]{3,2,1,0:T(8,128)(2,1)S(1)} %get-tuple-element.16), channel_id=1, source_target_pairs={{0,1},{1,2},{2,3},{3,0},{4,5},{5,6},{6,7},{7,4},{8,9},{9,10},{10,1... | collective-permute-start | bytes 786440 | tf_op jit(solution)/shard_map/ppermute | solution.py:18
  50.3 7.6 %collective-permute-start.14 = (bf16[2,8,16,512]{3,2,1,0:T(8,128)(2,1)S(1)}, bf16[2,8,16,512]{3,2,1,0:T(8,128)(2,1)S(1)}, u32[]{:S(2)}, u32[]{:S(2)}) collective-permute-start(bf16[2,8,16,512]{3,2,1,0:T(8,128)(2,1)S(1)} %get-tuple-element.17), channel_id=1, source_target_pairs={{0,3},{1,0},{2,1},{3,2},{4,7},{5,4},{6,5},{7,6},{8,11},{9,8},{10,9... | collective-permute-start | bytes 786440 | tf_op jit(solution)/shard_map/ppermute | solution.py:18

commit v4 on v3

--- a/solution.py
+++ b/solution.py
@@ -8,7 +8,7 @@
 from jax.sharding import Mesh, PartitionSpec as P
 
 ROW, COL = ("zlo", "core"), ("y", "zhi", "x")
-TILE = 256
+TILE = 512
 TILES = 1024 // TILE
 STEP = 64
 NEAR = (0, 3, 1, 2)

time: 61.2 us -> 60.9 us (level)
  Pallas kernels: 13.9 us -> 11.4 us
  waiting for transfers between devices: 8.62 us -> 10.9 us
    ppermute x14, waiting for transfers between devices: 6.6 us -> 8.84 us  [send(): return lax.ppermute(block, axis, [(i, (i + shift) % 4) for i in range(4)])]
    pallas_call x1, Pallas kernels: 7.75 us -> 5.61 us  [on_device(): pl.pallas_call(own_kernel, in_specs=[IN_VMEM] * 2 + [IN_SMEM, IN_HBM] + [...]
  transfers between devices with their start and end apart: 15 -> 15, of which waited for: 6 -> 6; matrix products, arithmetic and copies ran while one was open for 0% -> 0% of each run, Pallas kernels for 19% -> 15%
where the time goes in v4:
time: 60.9 us; the launch traced here: 60.2 us
  starting transfers between devices  24.7 us (41%)
  blocking collectives  12.8 us (21%)
  Pallas kernels  11.4 us (19%)
  waiting for transfers between devices  10.9 us (18%)
    ppermute x14, starting transfers between devices, send(): return lax.ppermute(block, axis, [(i, (i + shift) % 4) for i in range(4)])  20.1 us
    all_to_all x1, blocking collectives, on_device(): lax.all_to_all(amplitudes, ROW, split_axis=0, concat_axis=0, tiled=True)  12.8 us
    ppermute x14, waiting for transfers between devices, send(): return lax.ppermute(block, axis, [(i, (i + shift) % 4) for i in range(4)])  8.84 us
    pallas_call x2, Pallas kernels, more(): pl.pallas_call(functools.partial(more_kernel, groups), in_specs=[IN_VMEM]...  5.68 us
    pallas_call x1, Pallas kernels, on_device(): pl.pallas_call(own_kernel, in_specs=[IN_VMEM] * 2 + [IN_SMEM, IN_HBM] + [...  5.61 us
    ppermute x1, starting transfers between devices, on_device(): other = lax.ppermute(own, 'zhi', [(0, 1), (1, 0)])  4.57 us
    ppermute x1, waiting for transfers between devices, on_device(): other = lax.ppermute(own, 'zhi', [(0, 1), (1, 0)])  2.02 us
  transfers between devices with their start and end apart: 15, of which 6 were waited for; matrix products, arithmetic and copies ran while one was open for 0% of the time, Pallas kernels for 15%

profile of v4, /device:TPU:8, one launch (start us, length us, event | category | flops | bytes accessed | tf_op | source)
XLA Modules:
  0.0 60.2 jit_solution(11383954383615569987)
XLA Ops:
  0.0 12.8 %all_to_all.5 = bf16[8,16,512]{2,1,0:T(8,128)(2,1)S(1)} all-to-all(bf16[8,16,512]{2,1,0:T(8,128)(2,1)} %param.8), channel_id=1, replica_groups=mesh['zlo'=4,'core'=2,'y'=4,'zhi'=2,'x'=4] {'zlo','core'}, dimensions={0} | all-to-all | bytes 262144 | tf_op jit(solution)/shard_map/all_to_all | solution.py:188
  12.9 4.6 %collective-permute-start.5 = (bf16[8,16,512]{2,1,0:T(8,128)(2,1)S(1)}, bf16[8,16,512]{2,1,0:T(8,128)(2,1)S(1)}, u32[]{:S(2)}, u32[]{:S(2)}) collective-permute-start(bf16[8,16,512]{2,1,0:T(8,128)(2,1)S(1)} %all_to_all.5), channel_id=1, source_target_pairs={{0,4},{4,0},{1,5},{5,1},{2,6},{6,2},{3,7},{7,3},{8,12},{12,8},{9,1... | collective-permute-start | bytes 393224 | tf_op jit(solution)/shard_map/ppermute | solution.py:189
  17.4 3.0 %collective-permute-start.2 = (bf16[8,16,512]{2,1,0:T(8,128)(2,1)S(1)}, bf16[8,16,512]{2,1,0:T(8,128)(2,1)S(1)}, u32[]{:S(2)}, u32[]{:S(2)}) collective-permute-start(bf16[8,16,512]{2,1,0:T(8,128)(2,1)S(1)} %all_to_all.5), channel_id=1, source_target_pairs={{0,2},{1,3},{2,0},{3,1},{4,6},{5,7},{6,4},{7,5},{8,10},{9,11},{10,... | collective-permute-start | bytes 393224 | tf_op jit(solution)/shard_map/ppermute | solution.py:18
  20.5 1.1 %collective-permute-start.1 = (bf16[8,16,512]{2,1,0:T(8,128)(2,1)S(1)}, bf16[8,16,512]{2,1,0:T(8,128)(2,1)S(1)}, u32[]{:S(2)}, u32[]{:S(2)}) collective-permute-start(bf16[8,16,512]{2,1,0:T(8,128)(2,1)S(1)} %all_to_all.5), channel_id=1, source_target_pairs={{0,3},{1,0},{2,1},{3,2},{4,7},{5,4},{6,5},{7,6},{8,11},{9,8},{10,9... | collective-permute-start | bytes 393224 | tf_op jit(solution)/shard_map/ppermute | solution.py:18
  21.6 0.9 %collective-permute-start = (bf16[8,16,512]{2,1,0:T(8,128)(2,1)S(1)}, bf16[8,16,512]{2,1,0:T(8,128)(2,1)S(1)}, u32[]{:S(2)}, u32[]{:S(2)}) collective-permute-start(bf16[8,16,512]{2,1,0:T(8,128)(2,1)S(1)} %all_to_all.5), channel_id=1, source_target_pairs={{0,1},{1,2},{2,3},{3,0},{4,5},{5,6},{6,7},{7,4},{8,9},{9,10},{10,1... | collective-permute-start | bytes 393224 | tf_op jit(solution)/shard_map/ppermute | solution.py:18
  22.5 2.0 %collective-permute-done.5 = bf16[8,16,512]{2,1,0:T(8,128)(2,1)S(1)} collective-permute-done((bf16[8,16,512]{2,1,0:T(8,128)(2,1)S(1)}, bf16[8,16,512]{2,1,0:T(8,128)(2,1)S(1)}, u32[]{:S(2)}, u32[]{:S(2)}) %collective-permute-start.5) | collective-permute-done | bytes 131104 | tf_op jit(solution)/shard_map/ppermute | solution.py:189
  24.5 2.3 %collective-permute-start.8 = (bf16[8,16,512]{2,1,0:T(8,128)(2,1)S(1)}, bf16[8,16,512]{2,1,0:T(8,128)(2,1)S(1)}, u32[]{:S(2)}, u32[]{:S(2)}) collective-permute-start(bf16[8,16,512]{2,1,0:T(8,128)(2,1)S(1)} %collective-permute-done.5), channel_id=1, source_target_pairs={{0,16},{8,24},{16,0},{24,8},{1,17},{9,25},{17,1},{25,9},{2,18},{10... | collective-permute-start | bytes 393224 | tf_op jit(solution)/shard_map/ppermute | solution.py:18
  26.8 1.3 %collective-permute-start.7 = (bf16[8,16,512]{2,1,0:T(8,128)(2,1)S(1)}, bf16[8,16,512]{2,1,0:T(8,128)(2,1)S(1)}, u32[]{:S(2)}, u32[]{:S(2)}) collective-permute-start(bf16[8,16,512]{2,1,0:T(8,128)(2,1)S(1)} %collective-permute-done.5), channel_id=1, source_target_pairs={{0,24},{8,0},{16,8},{24,16},{1,25},{9,1},{17,9},{25,17},{2,26},{10... | collective-permute-start | bytes 393224 | tf_op jit(solution)/shard_map/ppermute | solution.py:18
  28.1 0.7 %collective-permute-start.6 = (bf16[8,16,512]{2,1,0:T(8,128)(2,1)S(1)}, bf16[8,16,512]{2,1,0:T(8,128)(2,1)S(1)}, u32[]{:S(2)}, u32[]{:S(2)}) collective-permute-start(bf16[8,16,512]{2,1,0:T(8,128)(2,1)S(1)} %collective-permute-done.5), channel_id=1, source_target_pairs={{0,8},{8,16},{16,24},{24,0},{1,9},{9,17},{17,25},{25,1},{2,10},{10... | collective-permute-start | bytes 393224 | tf_op jit(solution)/shard_map/ppermute | solution.py:18
  28.8 0.1 pad_maximum_fusion.refs_0_
  28.9 1.4 %collective-permute-start.4 = (bf16[4,8,16,512]{3,2,1,0:T(8,128)(2,1)S(1)}, bf16[4,8,16,512]{3,2,1,0:T(8,128)(2,1)S(1)}, u32[]{:S(2)}, u32[]{:S(2)}) collective-permute-start(bf16[4,8,16,512]{3,2,1,0:T(8,128)(2,1)S(1)} %pad_maximum_fusion.refs_0_), channel_id=1, source_target_pairs={{0,24},{8,0},{16,8},{24,16},{1,25},{9,1},{17,9},{25,17},{2,26},{10... | collective-permute-start | bytes 1572872 | tf_op jit(solution)/shard_map/ppermute | solution.py:18
  30.3 0.7 %collective-permute-start.3 = (bf16[4,8,16,512]{3,2,1,0:T(8,128)(2,1)S(1)}, bf16[4,8,16,512]{3,2,1,0:T(8,128)(2,1)S(1)}, u32[]{:S(2)}, u32[]{:S(2)}) collective-permute-start(bf16[4,8,16,512]{3,2,1,0:T(8,128)(2,1)S(1)} %pad_maximum_fusion.refs_0_), channel_id=1, source_target_pairs={{0,8},{8,16},{16,24},{24,0},{1,9},{9,17},{17,25},{25,1},{2,10},{10... | collective-permute-start | bytes 1572872 | tf_op jit(solution)/shard_map/ppermute | solution.py:18
  31.0 1.3 %collective-permute-done.8 = bf16[8,16,512]{2,1,0:T(8,128)(2,1)S(1)} collective-permute-done((bf16[8,16,512]{2,1,0:T(8,128)(2,1)S(1)}, bf16[8,16,512]{2,1,0:T(8,128)(2,1)S(1)}, u32[]{:S(2)}, u32[]{:S(2)}) %collective-permute-start.8) | collective-permute-done | bytes 131104 | tf_op jit(solution)/shard_map/ppermute | solution.py:18
  32.3 1.9 %collective-permute-done.7 = bf16[8,16,512]{2,1,0:T(8,128)(2,1)S(1)} collective-permute-done((bf16[8,16,512]{2,1,0:T(8,128)(2,1)S(1)}, bf16[8,16,512]{2,1,0:T(8,128)(2,1)S(1)}, u32[]{:S(2)}, u32[]{:S(2)}) %collective-permute-start.7) | collective-permute-done | bytes 131104 | tf_op jit(solution)/shard_map/ppermute | solution.py:18
  34.2 0.8 %collective-permute-done.6 = bf16[8,16,512]{2,1,0:T(8,128)(2,1)S(1)} collective-permute-done((bf16[8,16,512]{2,1,0:T(8,128)(2,1)S(1)}, bf16[8,16,512]{2,1,0:T(8,128)(2,1)S(1)}, u32[]{:S(2)}, u32[]{:S(2)}) %collective-permute-start.6) | collective-permute-done | bytes 131104 | tf_op jit(solution)/shard_map/ppermute | solution.py:18
  35.0 0.1 pad_maximum_fusion.1.refs_1_
  35.1 3.0 %collective-permute-start.12 = (bf16[4,8,16,512]{3,2,1,0:T(8,128)(2,1)S(1)}, bf16[4,8,16,512]{3,2,1,0:T(8,128)(2,1)S(1)}, u32[]{:S(2)}, u32[]{:S(2)}) collective-permute-start(bf16[4,8,16,512]{3,2,1,0:T(8,128)(2,1)S(1)} %pad_maximum_fusion.1.refs_1_), channel_id=1, source_target_pairs={{0,3},{1,0},{2,1},{3,2},{4,7},{5,4},{6,5},{7,6},{8,11},{9,8},{10,9... | collective-permute-start | bytes 1572872 | tf_op jit(solution)/shard_map/ppermute | solution.py:18
  38.1 0.0 collective-permute-start.11
  38.2 5.6 %shard_map.82 = (f32[1,512,1024]{2,1,0:T(8,128)}, bf16[4096,1024]{1,0:T(8,128)(2,1)S(1)}, f32[512,128]{1,0:T(8,128)S(1)}, f32[8,1024]{1,0:T(8,128)S(1)}) custom-call(bf16[4,8,16,512]{3,2,1,0:T(8,128)(2,1)S(1)} %pad_maximum_fusion.refs_0_, bf16[4,8,16,512]{3,2,1,0:T(8,128)(2,1)S(1)} %pad_maximum_fusion.1.refs_1_, s32[8]{0:T(128)S(1)} %copy-done.3, ...), custom_call_target="tpu_custom_call" | custom-call | tf_op jit(solution)/shard_map/pallas_call | solution.py:201
  43.8 0.0 collective-permute-done.4.ahead_ref.refs_1_
  43.8 0.0 collective-permute-done.3.back_ref.refs_0_
  43.9 0.9 %collective-permute-start.9 = (bf16[2,8,16,512]{3,2,1,0:T(8,128)(2,1)S(1)}, bf16[2,8,16,512]{3,2,1,0:T(8,128)(2,1)S(1)}, u32[]{:S(2)}, u32[]{:S(2)}) collective-permute-start(bf16[2,8,16,512]{3,2,1,0:T(8,128)(2,1)S(1)} %get-tuple-element.14), channel_id=1, source_target_pairs={{0,8},{8,16},{16,24},{24,0},{1,9},{9,17},{17,25},{25,1},{2,10},{10... | collective-permute-start | bytes 786440 | tf_op jit(solution)/shard_map/ppermute | solution.py:18
  44.8 1.2 %collective-permute-start.10 = (bf16[2,8,16,512]{3,2,1,0:T(8,128)(2,1)S(1)}, bf16[2,8,16,512]{3,2,1,0:T(8,128)(2,1)S(1)}, u32[]{:S(2)}, u32[]{:S(2)}) collective-permute-start(bf16[2,8,16,512]{3,2,1,0:T(8,128)(2,1)S(1)} %get-tuple-element.15), channel_id=1, source_target_pairs={{0,24},{8,0},{16,8},{24,16},{1,25},{9,1},{17,9},{25,17},{2,26},{10... | collective-permute-start | bytes 786440 | tf_op jit(solution)/shard_map/ppermute | solution.py:18
  46.0 0.0 collective-permute-done.12.ahead_ref.refs_3_
  46.0 4.0 %collective-permute-done.11.back_ref.refs_2_ = bf16[4,8,16,512]{3,2,1,0:T(8,128)(2,1)S(1)} collective-permute-done((bf16[4,8,16,512]{3,2,1,0:T(8,128)(2,1)S(1)}, bf16[4,8,16,512]{3,2,1,0:T(8,128)(2,1)S(1)}, u32[]{:S(2)}, u32[]{:S(2)}) %collective-permute-start.11) | collective-permute-done | bytes 524320 | tf_op jit(solution)/shard_map/ppermute | solution.py:18
  50.1 0.3 collective-permute-start.13
  50.3 3.2 %collective-permute-start.14 = (bf16[2,8,16,512]{3,2,1,0:T(8,128)(2,1)S(1)}, bf16[2,8,16,512]{3,2,1,0:T(8,128)(2,1)S(1)}, u32[]{:S(2)}, u32[]{:S(2)}) collective-permute-start(bf16[2,8,16,512]{3,2,1,0:T(8,128)(2,1)S(1)} %get-tuple-element.17), channel_id=1, source_target_pairs={{0,3},{1,0},{2,1},{3,2},{4,7},{5,4},{6,5},{7,6},{8,11},{9,8},{10,9... | collective-permute-start | bytes 786440 | tf_op jit(solution)/shard_map/ppermute | solution.py:18
  53.6 3.6 %shard_map.85.refs_8_ = f32[1,512,1024]{2,1,0:T(8,128)} custom-call(bf16[4,8,16,512]{3,2,1,0:T(8,128)(2,1)S(1)} %collective-permute-done.3.back_ref.refs_0_, bf16[4,8,16,512]{3,2,1,0:T(8,128)(2,1)S(1)} %collective-permute-done.4.ahead_ref.refs_1_, ...), custom_call_target="tpu_custom_call", output_to_operand_aliasing={{}: (8, {})} | custom-call | tf_op jit(solution)/shard_map/pallas_call | solution.py:163
  57.1 0.0 collective-permute-done.9.refs_0_
  57.1 0.0 collective-permute-done.10.refs_1_
  57.1 0.8 %collective-permute-done.13.refs_2_ = bf16[2,8,16,512]{3,2,1,0:T(8,128)(2,1)S(1)} collective-permute-done((bf16[2,8,16,512]{3,2,1,0:T(8,128)(2,1)S(1)}, bf16[2,8,16,512]{3,2,1,0:T(8,128)(2,1)S(1)}, u32[]{:S(2)}, u32[]{:S(2)}) %collective-permute-start.13) | collective-permute-done | bytes 262176 | tf_op jit(solution)/shard_map/ppermute | solution.py:18
  57.9 2.1 %shard_map.86 = f32[1,512,1024]{2,1,0:T(8,128)} custom-call(bf16[2,8,16,512]{3,2,1,0:T(8,128)(2,1)S(1)} %collective-permute-done.9.refs_0_, bf16[2,8,16,512]{3,2,1,0:T(8,128)(2,1)S(1)} %collective-permute-done.10.refs_1_, bf16[2,8,16,512]{3,2,1,0:T(8,128)(2,1)S(1)} %collective-permute-done.13.refs_2_, ...), custom_call_target="tpu_custom_call", output_to_operand_aliasing={{}: (8, {})} | custom-call | tf_op jit(solution)/shard_map/pallas_call | solution.py:163
  (20 shorter events, 0.1 us)
Async XLA Ops:
  0.0 38.1 %copy-start.5 = (f32[200]{0:T(256)S(1)}, f32[200]{0:T(256)}, u32[]{:S(2)}) copy-start(f32[200]{0:T(256)} %param.14) | copy-start | bytes 2404
  0.0 38.2 %copy-start.4 = (f32[1800]{0:T(1024)S(1)}, f32[1800]{0:T(1024)}, u32[]{:S(2)}) copy-start(f32[1800]{0:T(1024)} %param.15) | copy-start | bytes 21604
  0.0 38.2 %copy-start = (bf16[1,512,1024]{2,1,0:T(8,128)(2,1)S(1)}, bf16[1,512,1024]{2,1,0:T(8,128)(2,1)}, u32[]{:S(2)}) copy-start(bf16[1,512,1024]{2,1,0:T(8,128)(2,1)} %refs_5_.5) | copy-start | bytes 3145732
  0.0 38.2 %copy-start.1 = (s32[1,2,1024]{2,1,0:T(2,128)S(1)}, s32[1,2,1024]{2,1,0:T(2,128)}, u32[]{:S(2)}) copy-start(s32[1,2,1024]{2,1,0:T(2,128)} %refs_6_.1) | copy-start | bytes 24580
  0.0 38.2 %copy-start.2 = (s32[1,2,512]{2,1,0:T(2,128)S(1)}, s32[1,2,512]{2,1,0:T(2,128)}, u32[]{:S(2)}) copy-start(s32[1,2,512]{2,1,0:T(2,128)} %refs_5_.3) | copy-start | bytes 12292
  0.0 38.2 %copy-start.3 = (s32[8]{0:T(128)S(1)}, s32[8]{0:T(128)}, u32[]{:S(2)}) copy-start(s32[8]{0:T(128)} %refs_2_.1) | copy-start | bytes 100
  12.9 11.6 %collective-permute-start.5 = (bf16[8,16,512]{2,1,0:T(8,128)(2,1)S(1)}, bf16[8,16,512]{2,1,0:T(8,128)(2,1)S(1)}, u32[]{:S(2)}, u32[]{:S(2)}) collective-permute-start(bf16[8,16,512]{2,1,0:T(8,128)(2,1)S(1)} %all_to_all.5), channel_id=1, source_target_pairs={{0,4},{4,0},{1,5},{5,1},{2,6},{6,2},{3,7},{7,3},{8,12},{12,8},{9,1... | collective-permute-start | bytes 393224 | tf_op jit(solution)/shard_map/ppermute | solution.py:189
  17.4 10.7 %collective-permute-start.2 = (bf16[8,16,512]{2,1,0:T(8,128)(2,1)S(1)}, bf16[8,16,512]{2,1,0:T(8,128)(2,1)S(1)}, u32[]{:S(2)}, u32[]{:S(2)}) collective-permute-start(bf16[8,16,512]{2,1,0:T(8,128)(2,1)S(1)} %all_to_all.5), channel_id=1, source_target_pairs={{0,2},{1,3},{2,0},{3,1},{4,6},{5,7},{6,4},{7,5},{8,10},{9,11},{10,... | collective-permute-start | bytes 393224 | tf_op jit(solution)/shard_map/ppermute | solution.py:18
  20.5 8.4 %collective-permute-start.1 = (bf16[8,16,512]{2,1,0:T(8,128)(2,1)S(1)}, bf16[8,16,512]{2,1,0:T(8,128)(2,1)S(1)}, u32[]{:S(2)}, u32[]{:S(2)}) collective-permute-start(bf16[8,16,512]{2,1,0:T(8,128)(2,1)S(1)} %all_to_all.5), channel_id=1, source_target_pairs={{0,3},{1,0},{2,1},{3,2},{4,7},{5,4},{6,5},{7,6},{8,11},{9,8},{10,9... | collective-permute-start | bytes 393224 | tf_op jit(solution)/shard_map/ppermute | solution.py:18
  21.6 7.2 %collective-permute-start = (bf16[8,16,512]{2,1,0:T(8,128)(2,1)S(1)}, bf16[8,16,512]{2,1,0:T(8,128)(2,1)S(1)}, u32[]{:S(2)}, u32[]{:S(2)}) collective-permute-start(bf16[8,16,512]{2,1,0:T(8,128)(2,1)S(1)} %all_to_all.5), channel_id=1, source_target_pairs={{0,1},{1,2},{2,3},{3,0},{4,5},{5,6},{6,7},{7,4},{8,9},{9,10},{10,1... | collective-permute-start | bytes 393224 | tf_op jit(solution)/shard_map/ppermute | solution.py:18
  24.5 7.8 %collective-permute-start.8 = (bf16[8,16,512]{2,1,0:T(8,128)(2,1)S(1)}, bf16[8,16,512]{2,1,0:T(8,128)(2,1)S(1)}, u32[]{:S(2)}, u32[]{:S(2)}) collective-permute-start(bf16[8,16,512]{2,1,0:T(8,128)(2,1)S(1)} %collective-permute-done.5), channel_id=1, source_target_pairs={{0,16},{8,24},{16,0},{24,8},{1,17},{9,25},{17,1},{25,9},{2,18},{10... | collective-permute-start | bytes 393224 | tf_op jit(solution)/shard_map/ppermute | solution.py:18
  26.8 7.4 %collective-permute-start.7 = (bf16[8,16,512]{2,1,0:T(8,128)(2,1)S(1)}, bf16[8,16,512]{2,1,0:T(8,128)(2,1)S(1)}, u32[]{:S(2)}, u32[]{:S(2)}) collective-permute-start(bf16[8,16,512]{2,1,0:T(8,128)(2,1)S(1)} %collective-permute-done.5), channel_id=1, source_target_pairs={{0,24},{8,0},{16,8},{24,16},{1,25},{9,1},{17,9},{25,17},{2,26},{10... | collective-permute-start | bytes 393224 | tf_op jit(solution)/shard_map/ppermute | solution.py:18
  28.1 6.9 %collective-permute-start.6 = (bf16[8,16,512]{2,1,0:T(8,128)(2,1)S(1)}, bf16[8,16,512]{2,1,0:T(8,128)(2,1)S(1)}, u32[]{:S(2)}, u32[]{:S(2)}) collective-permute-start(bf16[8,16,512]{2,1,0:T(8,128)(2,1)S(1)} %collective-permute-done.5), channel_id=1, source_target_pairs={{0,8},{8,16},{16,24},{24,0},{1,9},{9,17},{17,25},{25,1},{2,10},{10... | collective-permute-start | bytes 393224 | tf_op jit(solution)/shard_map/ppermute | solution.py:18
  28.9 14.9 %collective-permute-start.4 = (bf16[4,8,16,512]{3,2,1,0:T(8,128)(2,1)S(1)}, bf16[4,8,16,512]{3,2,1,0:T(8,128)(2,1)S(1)}, u32[]{:S(2)}, u32[]{:S(2)}) collective-permute-start(bf16[4,8,16,512]{3,2,1,0:T(8,128)(2,1)S(1)} %pad_maximum_fusion.refs_0_), channel_id=1, source_target_pairs={{0,24},{8,0},{16,8},{24,16},{1,25},{9,1},{17,9},{25,17},{2,26},{10... | collective-permute-start | bytes 1572872 | tf_op jit(solution)/shard_map/ppermute | solution.py:18
  30.3 13.5 %collective-permute-start.3 = (bf16[4,8,16,512]{3,2,1,0:T(8,128)(2,1)S(1)}, bf16[4,8,16,512]{3,2,1,0:T(8,128)(2,1)S(1)}, u32[]{:S(2)}, u32[]{:S(2)}) collective-permute-start(bf16[4,8,16,512]{3,2,1,0:T(8,128)(2,1)S(1)} %pad_maximum_fusion.refs_0_), channel_id=1, source_target_pairs={{0,8},{8,16},{16,24},{24,0},{1,9},{9,17},{17,25},{25,1},{2,10},{10... | collective-permute-start | bytes 1572872 | tf_op jit(solution)/shard_map/ppermute | solution.py:18
  35.1 10.9 %collective-permute-start.12 = (bf16[4,8,16,512]{3,2,1,0:T(8,128)(2,1)S(1)}, bf16[4,8,16,512]{3,2,1,0:T(8,128)(2,1)S(1)}, u32[]{:S(2)}, u32[]{:S(2)}) collective-permute-start(bf16[4,8,16,512]{3,2,1,0:T(8,128)(2,1)S(1)} %pad_maximum_fusion.1.refs_1_), channel_id=1, source_target_pairs={{0,3},{1,0},{2,1},{3,2},{4,7},{5,4},{6,5},{7,6},{8,11},{9,8},{10,9... | collective-permute-start | bytes 1572872 | tf_op jit(solution)/shard_map/ppermute | solution.py:18
  38.1 11.9 %collective-permute-start.11 = (bf16[4,8,16,512]{3,2,1,0:T(8,128)(2,1)S(1)}, bf16[4,8,16,512]{3,2,1,0:T(8,128)(2,1)S(1)}, u32[]{:S(2)}, u32[]{:S(2)}) collective-permute-start(bf16[4,8,16,512]{3,2,1,0:T(8,128)(2,1)S(1)} %pad_maximum_fusion.1.refs_1_), channel_id=1, source_target_pairs={{0,1},{1,2},{2,3},{3,0},{4,5},{5,6},{6,7},{7,4},{8,9},{9,10},{10,1... | collective-permute-start | bytes 1572872 | tf_op jit(solution)/shard_map/ppermute | solution.py:18
  43.9 13.2 %collective-permute-start.9 = (bf16[2,8,16,512]{3,2,1,0:T(8,128)(2,1)S(1)}, bf16[2,8,16,512]{3,2,1,0:T(8,128)(2,1)S(1)}, u32[]{:S(2)}, u32[]{:S(2)}) collective-permute-start(bf16[2,8,16,512]{3,2,1,0:T(8,128)(2,1)S(1)} %get-tuple-element.14), channel_id=1, source_target_pairs={{0,8},{8,16},{16,24},{24,0},{1,9},{9,17},{17,25},{25,1},{2,10},{10... | collective-permute-start | bytes 786440 | tf_op jit(solution)/shard_map/ppermute | solution.py:18
  44.8 12.4 %collective-permute-start.10 = (bf16[2,8,16,512]{3,2,1,0:T(8,128)(2,1)S(1)}, bf16[2,8,16,512]{3,2,1,0:T(8,128)(2,1)S(1)}, u32[]{:S(2)}, u32[]{:S(2)}) collective-permute-start(bf16[2,8,16,512]{3,2,1,0:T(8,128)(2,1)S(1)} %get-tuple-element.15), channel_id=1, source_target_pairs={{0,24},{8,0},{16,8},{24,16},{1,25},{9,1},{17,9},{25,17},{2,26},{10... | collective-permute-start | bytes 786440 | tf_op jit(solution)/shard_map/ppermute | solution.py:18
  50.1 7.8 %collective-permute-start.13 = (bf16[2,8,16,512]{3,2,1,0:T(8,128)(2,1)S(1)}, bf16[2,8,16,512]{3,2,1,0:T(8,128)(2,1)S(1)}, u32[]{:S(2)}, u32[]{:S(2)}) collective-permute-start(bf16[2,8,16,512]{3,2,1,0:T(8,128)(2,1)S(1)} %get-tuple-element.16), channel_id=1, source_target_pairs={{0,1},{1,2},{2,3},{3,0},{4,5},{5,6},{6,7},{7,4},{8,9},{9,10},{10,1... | collective-permute-start | bytes 786440 | tf_op jit(solution)/shard_map/ppermute | solution.py:18
  50.3 7.6 %collective-permute-start.14 = (bf16[2,8,16,512]{3,2,1,0:T(8,128)(2,1)S(1)}, bf16[2,8,16,512]{3,2,1,0:T(8,128)(2,1)S(1)}, u32[]{:S(2)}, u32[]{:S(2)}) collective-permute-start(bf16[2,8,16,512]{3,2,1,0:T(8,128)(2,1)S(1)} %get-tuple-element.17), channel_id=1, source_target_pairs={{0,3},{1,0},{2,1},{3,2},{4,7},{5,4},{6,5},{7,6},{8,11},{9,8},{10,9... | collective-permute-start | bytes 786440 | tf_op jit(solution)/shard_map/ppermute | solution.py:18

commit v5 on v4

--- a/solution.py
+++ b/solution.py
@@ -218,7 +218,8 @@
     )
     far = []
     for half, axis in enumerate(("y", "x")):
-        low, high = relayed(beside[half * 2], beside[half * 2 + 1], vir_sum)
+        back, ahead = beside[half * 2 : half * 2 + 2]
+        low, high = (back[:2], ahead[2:]) if half else relayed(back, ahead, vir_sum)
         far += [send(low, axis, 1), send(high, axis, -1)]
     begun = more(BESIDE, beside, held, bare, occ_sum, vir_sum, begun)
     return more(FAR, far, held, bare, occ_sum, vir_sum, begun)

time: 60.9 us -> 59 us (0.969)
  waiting for transfers between devices: 10.9 us -> 7.79 us
    ppermute x14, waiting for transfers between devices: 8.84 us -> 5.77 us  [send(): return lax.ppermute(block, axis, [(i, (i + shift) % 4) for i in range(4)])]
    ppermute x14, starting transfers between devices: 20.1 us -> 20.7 us  [send(): return lax.ppermute(block, axis, [(i, (i + shift) % 4) for i in range(4)])]
  transfers between devices with their start and end apart: 15 -> 15, of which waited for: 6 -> 5; matrix products, arithmetic and copies ran while one was open for 0% -> 0% of each run, Pallas kernels for 15% -> 16%
where the time goes in v5:
time: 59 us; the launch traced here: 58 us
  starting transfers between devices  25.3 us (43%)
  blocking collectives  12.8 us (22%)
  Pallas kernels  11.5 us (19%)
  waiting for transfers between devices  7.79 us (13%)
    ppermute x14, starting transfers between devices, send(): return lax.ppermute(block, axis, [(i, (i + shift) % 4) for i in range(4)])  20.7 us
    all_to_all x1, blocking collectives, on_device(): lax.all_to_all(amplitudes, ROW, split_axis=0, concat_axis=0, tiled=True)  12.8 us
    pallas_call x1, Pallas kernels, on_device(): pl.pallas_call(own_kernel, in_specs=[IN_VMEM] * 2 + [IN_SMEM, IN_HBM] + [...  5.8 us
    ppermute x14, waiting for transfers between devices, send(): return lax.ppermute(block, axis, [(i, (i + shift) % 4) for i in range(4)])  5.77 us
    pallas_call x2, Pallas kernels, more(): pl.pallas_call(functools.partial(more_kernel, groups), in_specs=[IN_VMEM]...  5.68 us
    ppermute x1, starting transfers between devices, on_device(): other = lax.ppermute(own, 'zhi', [(0, 1), (1, 0)])  4.57 us
    ppermute x1, waiting for transfers between devices, on_device(): other = lax.ppermute(own, 'zhi', [(0, 1), (1, 0)])  2.02 us
  transfers between devices with their start and end apart: 15, of which 5 were waited for; matrix products, arithmetic and copies ran while one was open for 0% of the time, Pallas kernels for 16%

profile of v5, /device:TPU:8, one launch (start us, length us, event | category | flops | bytes accessed | tf_op | source)
XLA Modules:
  0.0 58.0 jit_solution(5607001091099988930)
XLA Ops:
  0.0 12.8 %all_to_all.5 = bf16[8,16,512]{2,1,0:T(8,128)(2,1)S(1)} all-to-all(bf16[8,16,512]{2,1,0:T(8,128)(2,1)} %param.8), channel_id=1, replica_groups=mesh['zlo'=4,'core'=2,'y'=4,'zhi'=2,'x'=4] {'zlo','core'}, dimensions={0} | all-to-all | bytes 262144 | tf_op jit(solution)/shard_map/all_to_all | solution.py:188
  12.9 4.6 %collective-permute-start.5 = (bf16[8,16,512]{2,1,0:T(8,128)(2,1)S(1)}, bf16[8,16,512]{2,1,0:T(8,128)(2,1)S(1)}, u32[]{:S(2)}, u32[]{:S(2)}) collective-permute-start(bf16[8,16,512]{2,1,0:T(8,128)(2,1)S(1)} %all_to_all.5), channel_id=1, source_target_pairs={{0,4},{4,0},{1,5},{5,1},{2,6},{6,2},{3,7},{7,3},{8,12},{12,8},{9,1... | collective-permute-start | bytes 393224 | tf_op jit(solution)/shard_map/ppermute | solution.py:189
  17.4 1.5 %collective-permute-start = (bf16[8,16,512]{2,1,0:T(8,128)(2,1)S(1)}, bf16[8,16,512]{2,1,0:T(8,128)(2,1)S(1)}, u32[]{:S(2)}, u32[]{:S(2)}) collective-permute-start(bf16[8,16,512]{2,1,0:T(8,128)(2,1)S(1)} %all_to_all.5), channel_id=1, source_target_pairs={{0,1},{1,2},{2,3},{3,0},{4,5},{5,6},{6,7},{7,4},{8,9},{9,10},{10,1... | collective-permute-start | bytes 393224 | tf_op jit(solution)/shard_map/ppermute | solution.py:18
  18.9 1.7 %collective-permute-start.1 = (bf16[8,16,512]{2,1,0:T(8,128)(2,1)S(1)}, bf16[8,16,512]{2,1,0:T(8,128)(2,1)S(1)}, u32[]{:S(2)}, u32[]{:S(2)}) collective-permute-start(bf16[8,16,512]{2,1,0:T(8,128)(2,1)S(1)} %all_to_all.5), channel_id=1, source_target_pairs={{0,3},{1,0},{2,1},{3,2},{4,7},{5,4},{6,5},{7,6},{8,11},{9,8},{10,9... | collective-permute-start | bytes 393224 | tf_op jit(solution)/shard_map/ppermute | solution.py:18
  20.7 1.8 %collective-permute-start.2 = (bf16[8,16,512]{2,1,0:T(8,128)(2,1)S(1)}, bf16[8,16,512]{2,1,0:T(8,128)(2,1)S(1)}, u32[]{:S(2)}, u32[]{:S(2)}) collective-permute-start(bf16[8,16,512]{2,1,0:T(8,128)(2,1)S(1)} %all_to_all.5), channel_id=1, source_target_pairs={{0,2},{1,3},{2,0},{3,1},{4,6},{5,7},{6,4},{7,5},{8,10},{9,11},{10,... | collective-permute-start | bytes 393224 | tf_op jit(solution)/shard_map/ppermute | solution.py:18
  22.5 2.0 %collective-permute-done.5 = bf16[8,16,512]{2,1,0:T(8,128)(2,1)S(1)} collective-permute-done((bf16[8,16,512]{2,1,0:T(8,128)(2,1)S(1)}, bf16[8,16,512]{2,1,0:T(8,128)(2,1)S(1)}, u32[]{:S(2)}, u32[]{:S(2)}) %collective-permute-start.5) | collective-permute-done | bytes 131104 | tf_op jit(solution)/shard_map/ppermute | solution.py:189
  24.5 1.6 %collective-permute-start.6 = (bf16[8,16,512]{2,1,0:T(8,128)(2,1)S(1)}, bf16[8,16,512]{2,1,0:T(8,128)(2,1)S(1)}, u32[]{:S(2)}, u32[]{:S(2)}) collective-permute-start(bf16[8,16,512]{2,1,0:T(8,128)(2,1)S(1)} %collective-permute-done.5), channel_id=1, source_target_pairs={{0,8},{8,16},{16,24},{24,0},{1,9},{9,17},{17,25},{25,1},{2,10},{10... | collective-permute-start | bytes 393224 | tf_op jit(solution)/shard_map/ppermute | solution.py:18
  26.1 0.4 collective-permute-start.7
  26.5 0.0 collective-permute-done
  26.5 2.3 %collective-permute-start.8 = (bf16[8,16,512]{2,1,0:T(8,128)(2,1)S(1)}, bf16[8,16,512]{2,1,0:T(8,128)(2,1)S(1)}, u32[]{:S(2)}, u32[]{:S(2)}) collective-permute-start(bf16[8,16,512]{2,1,0:T(8,128)(2,1)S(1)} %collective-permute-done.5), channel_id=1, source_target_pairs={{0,16},{8,24},{16,0},{24,8},{1,17},{9,25},{17,1},{25,9},{2,18},{10... | collective-permute-start | bytes 393224 | tf_op jit(solution)/shard_map/ppermute | solution.py:18
  28.8 0.1 pad_maximum_fusion.refs_0_
  28.9 0.9 %collective-permute-start.3 = (bf16[4,8,16,512]{3,2,1,0:T(8,128)(2,1)S(1)}, bf16[4,8,16,512]{3,2,1,0:T(8,128)(2,1)S(1)}, u32[]{:S(2)}, u32[]{:S(2)}) collective-permute-start(bf16[4,8,16,512]{3,2,1,0:T(8,128)(2,1)S(1)} %pad_maximum_fusion.refs_0_), channel_id=1, source_target_pairs={{0,8},{8,16},{16,24},{24,0},{1,9},{9,17},{17,25},{25,1},{2,10},{10... | collective-permute-start | bytes 1572872 | tf_op jit(solution)/shard_map/ppermute | solution.py:18
  29.8 1.2 %collective-permute-start.4 = (bf16[4,8,16,512]{3,2,1,0:T(8,128)(2,1)S(1)}, bf16[4,8,16,512]{3,2,1,0:T(8,128)(2,1)S(1)}, u32[]{:S(2)}, u32[]{:S(2)}) collective-permute-start(bf16[4,8,16,512]{3,2,1,0:T(8,128)(2,1)S(1)} %pad_maximum_fusion.refs_0_), channel_id=1, source_target_pairs={{0,24},{8,0},{16,8},{24,16},{1,25},{9,1},{17,9},{25,17},{2,26},{10... | collective-permute-start | bytes 1572872 | tf_op jit(solution)/shard_map/ppermute | solution.py:18
  31.0 0.0 collective-permute-done.6
  31.0 0.8 %collective-permute-done.7 = bf16[8,16,512]{2,1,0:T(8,128)(2,1)S(1)} collective-permute-done((bf16[8,16,512]{2,1,0:T(8,128)(2,1)S(1)}, bf16[8,16,512]{2,1,0:T(8,128)(2,1)S(1)}, u32[]{:S(2)}, u32[]{:S(2)}) %collective-permute-start.7) | collective-permute-done | bytes 131104 | tf_op jit(solution)/shard_map/ppermute | solution.py:18
  31.8 3.5 %collective-permute-done.8 = bf16[8,16,512]{2,1,0:T(8,128)(2,1)S(1)} collective-permute-done((bf16[8,16,512]{2,1,0:T(8,128)(2,1)S(1)}, bf16[8,16,512]{2,1,0:T(8,128)(2,1)S(1)}, u32[]{:S(2)}, u32[]{:S(2)}) %collective-permute-start.8) | collective-permute-done | bytes 131104 | tf_op jit(solution)/shard_map/ppermute | solution.py:18
  35.3 0.1 pad_maximum_fusion.1.refs_1_
  35.4 2.2 %collective-permute-start.11 = (bf16[4,8,16,512]{3,2,1,0:T(8,128)(2,1)S(1)}, bf16[4,8,16,512]{3,2,1,0:T(8,128)(2,1)S(1)}, u32[]{:S(2)}, u32[]{:S(2)}) collective-permute-start(bf16[4,8,16,512]{3,2,1,0:T(8,128)(2,1)S(1)} %pad_maximum_fusion.1.refs_1_), channel_id=1, source_target_pairs={{0,1},{1,2},{2,3},{3,0},{4,5},{5,6},{6,7},{7,4},{8,9},{9,10},{10,1... | collective-permute-start | bytes 1572872 | tf_op jit(solution)/shard_map/ppermute | solution.py:18
  37.6 1.4 %collective-permute-start.13 = (bf16[4,8,16,512]{3,2,1,0:T(8,128)(2,1)S(1)}, bf16[4,8,16,512]{3,2,1,0:T(8,128)(2,1)S(1)}, u32[]{:S(2)}, u32[]{:S(2)}) collective-permute-start(bf16[4,8,16,512]{3,2,1,0:T(8,128)(2,1)S(1)} %pad_maximum_fusion.1.refs_1_), channel_id=1, source_target_pairs={{0,3},{1,0},{2,1},{3,2},{4,7},{5,4},{6,5},{7,6},{8,11},{9,8},{10,9... | collective-permute-start | bytes 1572872 | tf_op jit(solution)/shard_map/ppermute | solution.py:18
  39.0 5.8 %shard_map.82 = (f32[1,512,1024]{2,1,0:T(8,128)}, bf16[4096,1024]{1,0:T(8,128)(2,1)S(1)}, f32[512,128]{1,0:T(8,128)S(1)}, f32[8,1024]{1,0:T(8,128)S(1)}) custom-call(bf16[4,8,16,512]{3,2,1,0:T(8,128)(2,1)S(1)} %pad_maximum_fusion.refs_0_, bf16[4,8,16,512]{3,2,1,0:T(8,128)(2,1)S(1)} %pad_maximum_fusion.1.refs_1_, s32[8]{0:T(128)S(1)} %copy-done.3, ...), custom_call_target="tpu_custom_call" | custom-call | tf_op jit(solution)/shard_map/pallas_call | solution.py:201
  44.8 0.0 collective-permute-done.3.back_ref.refs_0_
  44.9 0.0 collective-permute-done.4.ahead_ref.refs_1_
  44.9 0.6 %collective-permute-start.10 = (bf16[2,8,16,512]{3,2,1,0:T(8,128)(2,1)S(1)}, bf16[2,8,16,512]{3,2,1,0:T(8,128)(2,1)S(1)}, u32[]{:S(2)}, u32[]{:S(2)}) collective-permute-start(bf16[2,8,16,512]{3,2,1,0:T(8,128)(2,1)S(1)} %get-tuple-element.13), channel_id=1, source_target_pairs={{0,24},{8,0},{16,8},{24,16},{1,25},{9,1},{17,9},{25,17},{2,26},{10... | collective-permute-start | bytes 786440 | tf_op jit(solution)/shard_map/ppermute | solution.py:18
  45.5 1.5 %collective-permute-start.9 = (bf16[2,8,16,512]{3,2,1,0:T(8,128)(2,1)S(1)}, bf16[2,8,16,512]{3,2,1,0:T(8,128)(2,1)S(1)}, u32[]{:S(2)}, u32[]{:S(2)}) collective-permute-start(bf16[2,8,16,512]{3,2,1,0:T(8,128)(2,1)S(1)} %get-tuple-element.12), channel_id=1, source_target_pairs={{0,8},{8,16},{16,24},{24,0},{1,9},{9,17},{17,25},{25,1},{2,10},{10... | collective-permute-start | bytes 786440 | tf_op jit(solution)/shard_map/ppermute | solution.py:18
  47.0 0.0 collective-permute-done.11.refs_2_
  47.0 1.7 %collective-permute-start.12 = (bf16[2,8,16,512]{3,2,1,0:T(8,128)(2,1)S(1)}, bf16[2,8,16,512]{3,2,1,0:T(8,128)(2,1)S(1)}, u32[]{:S(2)}, u32[]{:S(2)}) collective-permute-start(bf16[2,8,16,512]{3,2,1,0:T(8,128)(2,1)S(1)} %slice.8), channel_id=1, source_target_pairs={{0,1},{1,2},{2,3},{3,0},{4,5},{5,6},{6,7},{7,4},{8,9},{9,10},{10,1... | collective-permute-start | bytes 786440 | tf_op jit(solution)/shard_map/ppermute | solution.py:18
  48.7 1.9 %collective-permute-start.14 = (bf16[2,8,16,512]{3,2,1,0:T(8,128)(2,1)S(1)}, bf16[2,8,16,512]{3,2,1,0:T(8,128)(2,1)S(1)}, u32[]{:S(2)}, u32[]{:S(2)}) collective-permute-start(bf16[2,8,16,512]{3,2,1,0:T(8,128)(2,1)S(1)} %slice.9), channel_id=1, source_target_pairs={{0,3},{1,0},{2,1},{3,2},{4,7},{5,4},{6,5},{7,6},{8,11},{9,8},{10,9... | collective-permute-start | bytes 786440 | tf_op jit(solution)/shard_map/ppermute | solution.py:18
  50.6 3.5 %shard_map.84.refs_8_ = f32[1,512,1024]{2,1,0:T(8,128)} custom-call(bf16[4,8,16,512]{3,2,1,0:T(8,128)(2,1)S(1)} %collective-permute-done.3.back_ref.refs_0_, bf16[4,8,16,512]{3,2,1,0:T(8,128)(2,1)S(1)} %collective-permute-done.4.ahead_ref.refs_1_, bf16[4,8,16,512]{3,2,1,0:T(8,128)(2,1)S(1)} %collective-permute-done.11.refs_2_, ...), custom_call_target="tpu_custom_call", output_to_operand_aliasing={{}: (8, {})} | custom-call | tf_op jit(solution)/shard_map/pallas_call | solution.py:163
  54.2 0.0 collective-permute-done.10.refs_1_
  54.2 0.7 %collective-permute-done.12.refs_2_ = bf16[2,8,16,512]{3,2,1,0:T(8,128)(2,1)S(1)} collective-permute-done((bf16[2,8,16,512]{3,2,1,0:T(8,128)(2,1)S(1)}, bf16[2,8,16,512]{3,2,1,0:T(8,128)(2,1)S(1)}, u32[]{:S(2)}, u32[]{:S(2)}) %collective-permute-start.12) | collective-permute-done | bytes 262176 | tf_op jit(solution)/shard_map/ppermute | solution.py:18
  54.9 0.7 %collective-permute-done.14.refs_3_ = bf16[2,8,16,512]{3,2,1,0:T(8,128)(2,1)S(1)} collective-permute-done((bf16[2,8,16,512]{3,2,1,0:T(8,128)(2,1)S(1)}, bf16[2,8,16,512]{3,2,1,0:T(8,128)(2,1)S(1)}, u32[]{:S(2)}, u32[]{:S(2)}) %collective-permute-start.14) | collective-permute-done | bytes 262176 | tf_op jit(solution)/shard_map/ppermute | solution.py:18
  55.6 2.2 %shard_map.85 = f32[1,512,1024]{2,1,0:T(8,128)} custom-call(bf16[2,8,16,512]{3,2,1,0:T(8,128)(2,1)S(1)} %collective-permute-done.9.refs_0_, bf16[2,8,16,512]{3,2,1,0:T(8,128)(2,1)S(1)} %collective-permute-done.10.refs_1_, bf16[2,8,16,512]{3,2,1,0:T(8,128)(2,1)S(1)} %collective-permute-done.12.refs_2_, ...), custom_call_target="tpu_custom_call", output_to_operand_aliasing={{}: (8, {})} | custom-call | tf_op jit(solution)/shard_map/pallas_call | solution.py:163
  (21 shorter events, 0.1 us)
Async XLA Ops:
  0.0 39.0 %copy-start.5 = (f32[200]{0:T(256)S(1)}, f32[200]{0:T(256)}, u32[]{:S(2)}) copy-start(f32[200]{0:T(256)} %param.14) | copy-start | bytes 2404
  0.0 39.0 %copy-start.4 = (f32[1800]{0:T(1024)S(1)}, f32[1800]{0:T(1024)}, u32[]{:S(2)}) copy-start(f32[1800]{0:T(1024)} %param.15) | copy-start | bytes 21604
  0.0 39.0 %copy-start = (bf16[1,512,1024]{2,1,0:T(8,128)(2,1)S(1)}, bf16[1,512,1024]{2,1,0:T(8,128)(2,1)}, u32[]{:S(2)}) copy-start(bf16[1,512,1024]{2,1,0:T(8,128)(2,1)} %refs_5_.5) | copy-start | bytes 3145732
  0.0 39.0 %copy-start.3 = (s32[8]{0:T(128)S(1)}, s32[8]{0:T(128)}, u32[]{:S(2)}) copy-start(s32[8]{0:T(128)} %refs_2_.1) | copy-start | bytes 100
  0.0 39.0 %copy-start.2 = (s32[1,2,512]{2,1,0:T(2,128)S(1)}, s32[1,2,512]{2,1,0:T(2,128)}, u32[]{:S(2)}) copy-start(s32[1,2,512]{2,1,0:T(2,128)} %refs_5_.3) | copy-start | bytes 12292
  0.0 39.0 %copy-start.1 = (s32[1,2,1024]{2,1,0:T(2,128)S(1)}, s32[1,2,1024]{2,1,0:T(2,128)}, u32[]{:S(2)}) copy-start(s32[1,2,1024]{2,1,0:T(2,128)} %refs_6_.1) | copy-start | bytes 24580
  12.9 11.6 %collective-permute-start.5 = (bf16[8,16,512]{2,1,0:T(8,128)(2,1)S(1)}, bf16[8,16,512]{2,1,0:T(8,128)(2,1)S(1)}, u32[]{:S(2)}, u32[]{:S(2)}) collective-permute-start(bf16[8,16,512]{2,1,0:T(8,128)(2,1)S(1)} %all_to_all.5), channel_id=1, source_target_pairs={{0,4},{4,0},{1,5},{5,1},{2,6},{6,2},{3,7},{7,3},{8,12},{12,8},{9,1... | collective-permute-start | bytes 393224 | tf_op jit(solution)/shard_map/ppermute | solution.py:189
  17.4 9.1 %collective-permute-start = (bf16[8,16,512]{2,1,0:T(8,128)(2,1)S(1)}, bf16[8,16,512]{2,1,0:T(8,128)(2,1)S(1)}, u32[]{:S(2)}, u32[]{:S(2)}) collective-permute-start(bf16[8,16,512]{2,1,0:T(8,128)(2,1)S(1)} %all_to_all.5), channel_id=1, source_target_pairs={{0,1},{1,2},{2,3},{3,0},{4,5},{5,6},{6,7},{7,4},{8,9},{9,10},{10,1... | collective-permute-start | bytes 393224 | tf_op jit(solution)/shard_map/ppermute | solution.py:18
  18.9 9.9 %collective-permute-start.1 = (bf16[8,16,512]{2,1,0:T(8,128)(2,1)S(1)}, bf16[8,16,512]{2,1,0:T(8,128)(2,1)S(1)}, u32[]{:S(2)}, u32[]{:S(2)}) collective-permute-start(bf16[8,16,512]{2,1,0:T(8,128)(2,1)S(1)} %all_to_all.5), channel_id=1, source_target_pairs={{0,3},{1,0},{2,1},{3,2},{4,7},{5,4},{6,5},{7,6},{8,11},{9,8},{10,9... | collective-permute-start | bytes 393224 | tf_op jit(solution)/shard_map/ppermute | solution.py:18
  20.7 8.2 %collective-permute-start.2 = (bf16[8,16,512]{2,1,0:T(8,128)(2,1)S(1)}, bf16[8,16,512]{2,1,0:T(8,128)(2,1)S(1)}, u32[]{:S(2)}, u32[]{:S(2)}) collective-permute-start(bf16[8,16,512]{2,1,0:T(8,128)(2,1)S(1)} %all_to_all.5), channel_id=1, source_target_pairs={{0,2},{1,3},{2,0},{3,1},{4,6},{5,7},{6,4},{7,5},{8,10},{9,11},{10,... | collective-permute-start | bytes 393224 | tf_op jit(solution)/shard_map/ppermute | solution.py:18
  24.5 6.5 %collective-permute-start.6 = (bf16[8,16,512]{2,1,0:T(8,128)(2,1)S(1)}, bf16[8,16,512]{2,1,0:T(8,128)(2,1)S(1)}, u32[]{:S(2)}, u32[]{:S(2)}) collective-permute-start(bf16[8,16,512]{2,1,0:T(8,128)(2,1)S(1)} %collective-permute-done.5), channel_id=1, source_target_pairs={{0,8},{8,16},{16,24},{24,0},{1,9},{9,17},{17,25},{25,1},{2,10},{10... | collective-permute-start | bytes 393224 | tf_op jit(solution)/shard_map/ppermute | solution.py:18
  26.1 5.7 %collective-permute-start.7 = (bf16[8,16,512]{2,1,0:T(8,128)(2,1)S(1)}, bf16[8,16,512]{2,1,0:T(8,128)(2,1)S(1)}, u32[]{:S(2)}, u32[]{:S(2)}) collective-permute-start(bf16[8,16,512]{2,1,0:T(8,128)(2,1)S(1)} %collective-permute-done.5), channel_id=1, source_target_pairs={{0,24},{8,0},{16,8},{24,16},{1,25},{9,1},{17,9},{25,17},{2,26},{10... | collective-permute-start | bytes 393224 | tf_op jit(solution)/shard_map/ppermute | solution.py:18
  26.5 8.8 %collective-permute-start.8 = (bf16[8,16,512]{2,1,0:T(8,128)(2,1)S(1)}, bf16[8,16,512]{2,1,0:T(8,128)(2,1)S(1)}, u32[]{:S(2)}, u32[]{:S(2)}) collective-permute-start(bf16[8,16,512]{2,1,0:T(8,128)(2,1)S(1)} %collective-permute-done.5), channel_id=1, source_target_pairs={{0,16},{8,24},{16,0},{24,8},{1,17},{9,25},{17,1},{25,9},{2,18},{10... | collective-permute-start | bytes 393224 | tf_op jit(solution)/shard_map/ppermute | solution.py:18
  28.9 15.9 %collective-permute-start.3 = (bf16[4,8,16,512]{3,2,1,0:T(8,128)(2,1)S(1)}, bf16[4,8,16,512]{3,2,1,0:T(8,128)(2,1)S(1)}, u32[]{:S(2)}, u32[]{:S(2)}) collective-permute-start(bf16[4,8,16,512]{3,2,1,0:T(8,128)(2,1)S(1)} %pad_maximum_fusion.refs_0_), channel_id=1, source_target_pairs={{0,8},{8,16},{16,24},{24,0},{1,9},{9,17},{17,25},{25,1},{2,10},{10... | collective-permute-start | bytes 1572872 | tf_op jit(solution)/shard_map/ppermute | solution.py:18
  29.8 15.0 %collective-permute-start.4 = (bf16[4,8,16,512]{3,2,1,0:T(8,128)(2,1)S(1)}, bf16[4,8,16,512]{3,2,1,0:T(8,128)(2,1)S(1)}, u32[]{:S(2)}, u32[]{:S(2)}) collective-permute-start(bf16[4,8,16,512]{3,2,1,0:T(8,128)(2,1)S(1)} %pad_maximum_fusion.refs_0_), channel_id=1, source_target_pairs={{0,24},{8,0},{16,8},{24,16},{1,25},{9,1},{17,9},{25,17},{2,26},{10... | collective-permute-start | bytes 1572872 | tf_op jit(solution)/shard_map/ppermute | solution.py:18
  35.4 11.6 %collective-permute-start.11 = (bf16[4,8,16,512]{3,2,1,0:T(8,128)(2,1)S(1)}, bf16[4,8,16,512]{3,2,1,0:T(8,128)(2,1)S(1)}, u32[]{:S(2)}, u32[]{:S(2)}) collective-permute-start(bf16[4,8,16,512]{3,2,1,0:T(8,128)(2,1)S(1)} %pad_maximum_fusion.1.refs_1_), channel_id=1, source_target_pairs={{0,1},{1,2},{2,3},{3,0},{4,5},{5,6},{6,7},{7,4},{8,9},{9,10},{10,1... | collective-permute-start | bytes 1572872 | tf_op jit(solution)/shard_map/ppermute | solution.py:18
  37.6 11.1 %collective-permute-start.13 = (bf16[4,8,16,512]{3,2,1,0:T(8,128)(2,1)S(1)}, bf16[4,8,16,512]{3,2,1,0:T(8,128)(2,1)S(1)}, u32[]{:S(2)}, u32[]{:S(2)}) collective-permute-start(bf16[4,8,16,512]{3,2,1,0:T(8,128)(2,1)S(1)} %pad_maximum_fusion.1.refs_1_), channel_id=1, source_target_pairs={{0,3},{1,0},{2,1},{3,2},{4,7},{5,4},{6,5},{7,6},{8,11},{9,8},{10,9... | collective-permute-start | bytes 1572872 | tf_op jit(solution)/shard_map/ppermute | solution.py:18
  44.9 9.3 %collective-permute-start.10 = (bf16[2,8,16,512]{3,2,1,0:T(8,128)(2,1)S(1)}, bf16[2,8,16,512]{3,2,1,0:T(8,128)(2,1)S(1)}, u32[]{:S(2)}, u32[]{:S(2)}) collective-permute-start(bf16[2,8,16,512]{3,2,1,0:T(8,128)(2,1)S(1)} %get-tuple-element.13), channel_id=1, source_target_pairs={{0,24},{8,0},{16,8},{24,16},{1,25},{9,1},{17,9},{25,17},{2,26},{10... | collective-permute-start | bytes 786440 | tf_op jit(solution)/shard_map/ppermute | solution.py:18
  45.5 8.6 %collective-permute-start.9 = (bf16[2,8,16,512]{3,2,1,0:T(8,128)(2,1)S(1)}, bf16[2,8,16,512]{3,2,1,0:T(8,128)(2,1)S(1)}, u32[]{:S(2)}, u32[]{:S(2)}) collective-permute-start(bf16[2,8,16,512]{3,2,1,0:T(8,128)(2,1)S(1)} %get-tuple-element.12), channel_id=1, source_target_pairs={{0,8},{8,16},{16,24},{24,0},{1,9},{9,17},{17,25},{25,1},{2,10},{10... | collective-permute-start | bytes 786440 | tf_op jit(solution)/shard_map/ppermute | solution.py:18
  47.0 7.8 %collective-permute-start.12 = (bf16[2,8,16,512]{3,2,1,0:T(8,128)(2,1)S(1)}, bf16[2,8,16,512]{3,2,1,0:T(8,128)(2,1)S(1)}, u32[]{:S(2)}, u32[]{:S(2)}) collective-permute-start(bf16[2,8,16,512]{3,2,1,0:T(8,128)(2,1)S(1)} %slice.8), channel_id=1, source_target_pairs={{0,1},{1,2},{2,3},{3,0},{4,5},{5,6},{6,7},{7,4},{8,9},{9,10},{10,1... | collective-permute-start | bytes 786440 | tf_op jit(solution)/shard_map/ppermute | solution.py:18
  48.7 6.9 %collective-permute-start.14 = (bf16[2,8,16,512]{3,2,1,0:T(8,128)(2,1)S(1)}, bf16[2,8,16,512]{3,2,1,0:T(8,128)(2,1)S(1)}, u32[]{:S(2)}, u32[]{:S(2)}) collective-permute-start(bf16[2,8,16,512]{3,2,1,0:T(8,128)(2,1)S(1)} %slice.9), channel_id=1, source_target_pairs={{0,3},{1,0},{2,1},{3,2},{4,7},{5,4},{6,5},{7,6},{8,11},{9,8},{10,9... | collective-permute-start | bytes 786440 | tf_op jit(solution)/shard_map/ppermute | solution.py:18
